TPU v7x, 256 devices: a whole 4x4x8 slice. The times are simulated.
256 devices in a mesh: seq: 16 (over y, x), row: 4 (over z_hi), col: 4 (over z_lo, core).
Axes of the slice: x: 4, y: 4, z: 8 (z_hi: 4, z_lo: 2; z = z_hi * 2 + z_lo), core: 2. Of those that a mesh axis runs over, the one named last changes fastest.
Arguments:
- alignment_input: bfloat16 [512, 256, 64], P('seq', ('row', 'col')), may hold values from -30 to 30
- pair_input: bfloat16 [256, 256, 128], P('row', 'col'), may hold values from -60 to 60
- token_valid_mask: int32 [256], replicated, may hold values from 0 to 1, as said below
- first_factor_weights: bfloat16 [64, 32], replicated, may hold values from -0.75 to 0.75
- second_factor_weights: bfloat16 [64, 32], replicated, may hold values from -0.75 to 0.75
- content_weights_grid: bfloat16 [64, 256], replicated, may hold values from -0.75 to 0.75
- sigmoid_weights_grid: bfloat16 [64, 256], replicated, may hold values from -0.75 to 0.75
- outer_matrix: float32 [1024, 128], replicated, may hold values from -0.0078125 to 0.0078125
- score_matrix: float32 [128, 8], replicated, may hold values from -20 to 20
- final_mixing_weights: bfloat16 [256, 64], replicated, may hold values from -0.375 to 0.375
- adjoint_of_rowset: bfloat16 [512, 256, 64], P('seq', ('row', 'col')), may hold values from -48 to 48
Outputs:
- alignment_output: bfloat16 [512, 256, 64], P('seq', ('row', 'col'))
- pair_output: bfloat16 [256, 256, 128], P('row', 'col')
- pair_gradient: bfloat16 [256, 256, 128], P('row', 'col')
Inputs may be any that keep to these rules, and one draw needn't show every extreme that they name: `token_valid_mask`: the mask is 1 on a first run of more than half of the 256 tokens and 0 on the rest.
All inputs are finite; a program needn't handle non-finite values.
Results may differ from a plain program's by a relative error of at most 0.028.
The roundings to bfloat16 on the way count: a program that leaves them out, or rounds other values in their place, can miss the bound.
Values may be sent and summed in bfloat16 or wider, within the bound.
A program may use at most 64 MiB of HBM per device.

v0:
```python
import math

import jax
import jax.numpy as jnp
from jax import lax
from jax.sharding import PartitionSpec as P

epsilon = 1e-05
far_below = -1e30


def layer_normalize(inputs):
    center = inputs - jnp.mean(inputs, axis=-1, keepdims=True)
    inverse = lax.rsqrt(jnp.mean(center * center, axis=-1, keepdims=True) + epsilon)
    return (center * inverse, inverse)


def on_device(
    alignment_input,
    pair_input,
    token_valid_mask,
    first_factor_weights,
    second_factor_weights,
    content_weights_grid,
    sigmoid_weights_grid,
    outer_matrix,
    score_matrix,
    final_mixing_weights,
    adjoint_of_rowset,
):
    highest = lax.Precision.HIGHEST
    count_col = lax.axis_size("col")
    row_index = lax.axis_index("row")
    col_index = lax.axis_index("col")
    local_sequences = alignment_input.shape[0]
    local_tokens = alignment_input.shape[1]
    tile_i = pair_input.shape[0]
    tile_j = pair_input.shape[1]
    head_count = score_matrix.shape[1]
    proj_width = second_factor_weights.shape[1]
    own_start = (row_index * count_col + col_index) * local_tokens
    own_mask = lax.dynamic_slice_in_dim(token_valid_mask, own_start, local_tokens).astype(
        jnp.float32
    )
    col_mask = lax.dynamic_slice_in_dim(token_valid_mask, col_index * tile_j, tile_j).astype(
        jnp.float32
    )
    normalized_pair = layer_normalize(alignment_input.astype(jnp.float32))[0].astype(jnp.bfloat16)
    left_proj = (
        jnp.dot(normalized_pair, first_factor_weights, preferred_element_type=jnp.float32)
        * own_mask[None, :, None]
    ).astype(jnp.bfloat16)
    right_proj = (
        jnp.dot(normalized_pair, second_factor_weights, preferred_element_type=jnp.float32)
        * own_mask[None, :, None]
    ).astype(jnp.bfloat16)
    values = jnp.dot(
        normalized_pair, content_weights_grid, preferred_element_type=jnp.float32
    ).astype(jnp.bfloat16)
    gating = jax.nn.sigmoid(
        jnp.dot(normalized_pair, sigmoid_weights_grid, preferred_element_type=jnp.float32)
    )
    joined = jnp.concatenate([right_proj, values], axis=2)
    rows_left = lax.all_gather(left_proj, "col", axis=1, tiled=True)
    every_joined = lax.all_gather(joined, ("row", "col"), axis=1, tiled=True)
    cols_joined = lax.dynamic_slice_in_dim(every_joined, col_index * tile_j, tile_j, 1)
    cols_right = cols_joined[:, :, :proj_width]
    cols_values = cols_joined[:, :, proj_width:]

    def outer_rows(row_start, row_count):
        rows_part = lax.dynamic_slice_in_dim(rows_left, row_start, row_count, 1)
        products = jnp.einsum(
            "sic,sjd->ijcd", rows_part, cols_right, preferred_element_type=jnp.float32
        )
        return products.reshape(row_count, tile_j, -1)

    pair_float = pair_input.astype(jnp.float32)
    block_rows = math.gcd(tile_i, 8)

    def one_block(number):
        return jnp.dot(
            outer_rows(0 + number * block_rows, block_rows),
            outer_matrix,
            precision=highest,
            preferred_element_type=jnp.float32,
        )

    pieces = lax.map(one_block, jnp.arange(tile_i // block_rows, dtype=jnp.int32))
    update = lax.psum(pieces.reshape(tile_i, tile_j, outer_matrix.shape[1]), "seq")
    pair_output = (pair_float + update).astype(jnp.bfloat16)
    normal_pair, inverse_pair = layer_normalize(pair_output.astype(jnp.float32))
    logits = jnp.dot(
        normal_pair, score_matrix, precision=highest, preferred_element_type=jnp.float32
    )
    valid_cols = col_mask[None, :, None] > 0
    masked = jnp.where(valid_cols, logits, far_below)
    local_peak = jnp.max(masked, axis=1)
    row_max = lax.pmax(local_peak, "col")
    scaled = jnp.exp(masked - row_max[:, None, :]) * col_mask[None, :, None]
    row_sum = lax.psum(jnp.sum(scaled, axis=1), "col")
    probabilities = scaled / row_sum[:, None, :]
    weights = probabilities.astype(jnp.bfloat16)
    head_values = cols_values.reshape(local_sequences, tile_j, head_count, -1)
    partial_value = jnp.einsum(
        "ijh,sjhk->sihk", weights, head_values, preferred_element_type=jnp.float32
    ).reshape(local_sequences, tile_i, -1)
    averaged = lax.psum_scatter(
        partial_value.astype(jnp.bfloat16), "col", scatter_dimension=1, tiled=True
    ).astype(jnp.float32)
    gated_values = (gating * averaged).astype(jnp.bfloat16)
    alignment_output = (
        alignment_input.astype(jnp.float32)
        + jnp.dot(gated_values, final_mixing_weights, preferred_element_type=jnp.float32)
    ).astype(jnp.bfloat16)
    gated_gradient = jnp.dot(
        adjoint_of_rowset, final_mixing_weights.T, preferred_element_type=jnp.float32
    )
    grad_avg = (gated_gradient * gating).astype(jnp.bfloat16)
    rows_grad = lax.all_gather(grad_avg, "col", axis=1, tiled=True)
    weight_part = jnp.einsum(
        "sihk,sjhk->ijh",
        rows_grad.reshape(local_sequences, tile_i, head_count, -1),
        head_values,
        preferred_element_type=jnp.float32,
    )
    grad_weights = lax.psum(weight_part.astype(jnp.bfloat16), "seq").astype(jnp.float32)
    inner_sum = lax.psum(jnp.sum(probabilities * grad_weights, axis=1), "col")
    grad_logits = probabilities * (grad_weights - inner_sum[:, None, :])
    grad_normal = jnp.dot(
        grad_logits, score_matrix.T, precision=highest, preferred_element_type=jnp.float32
    )
    centered_grad = grad_normal - jnp.mean(grad_normal, axis=-1, keepdims=True)
    along = jnp.mean(grad_normal * normal_pair, axis=-1, keepdims=True)
    pair_gradient = (inverse_pair * (centered_grad - normal_pair * along)).astype(jnp.bfloat16)
    return (alignment_output, pair_output, pair_gradient)


def solution(mesh):
    in_specs = (
        P("seq", ("row", "col"), None),
        P("row", "col", None),
        P(),
        P(),
        P(),
        P(),
        P(),
        P(),
        P(),
        P(),
        P("seq", ("row", "col"), None),
    )
    out_specs = (P("seq", ("row", "col"), None), P("row", "col", None), P("row", "col", None))
    return jax.shard_map(
        on_device, mesh=mesh, in_specs=in_specs, out_specs=out_specs, check_vma=False
    )
```

profile of v0, /device:TPU:1, one launch (start us, length us, event | category | flops | bytes accessed | tf_op | source)
XLA Modules:
  0.0 390.6 jit_solution(3369616235088897288)
XLA Ops:
  16.5 9.6 %all_gather.10 = bf16[32,64,32]{2,0,1:T(8,128)(2,1)S(1)} all-gather(bf16[32,16,32]{2,0,1:T(8,128)(2,1)S(1)} %fusion.29), channel_id=1, replica_groups=mesh['seq'=16,'row'=4,'col'=4] {'col'}, dimensions={1}, use_global_device_ids=true | all-gather | bytes 163840 | tf_op jit(solution)/shard_map/all_gather | solution.py:64
  26.1 38.5 %all-gather.3.cloned.1.call-done = bf16[32,256,288]{2,1,0:T(8,128)(2,1)} async-done(((bf16[32,16,288]{2,1,0:T(8,128)(2,1)}), bf16[32,256,288]{2,1,0:T(8,128)(2,1)}) %all-gather.3.cloned.1.call-update) | async-done | bytes 4718608 | tf_op jit(solution)/shard_map/all_gather | solution.py:65
  66.2 94.0 %while.10 = (s32[]{:T(128)}, f32[8,8,64,128]{3,2,1,0:T(8,128)}, s32[8]{0:T(128)S(1)}, bf16[32,64,32]{2,0,1:T(8,128)(2,1)S(1)}, bf16[32,64,32]{1,0,2:T(8,128)(2,1...) while((s32[]{:T(128)}, f32[8,8,64,128]{3,2,1,0:T(8,128)}, ...), condition=%wide.region_3.4_spmd, body=%wide.region_2.3_spmd.sunk | while | flops 838860800 | bytes 9502895 | solution.py:88
  70.5 7.4 %fusion.73 = f32[8,8,64,128]{3,2,1,0:T(8,128)} fusion(f32[8,8,64,128]{3,2,1,0:T(8,128)} %get-tuple-element.127, s32[]{:T(128)S(6)} %copy.77, f32[8,64,1024]{1,2,0:T(8,128)S(1)} %bitcast.81, f32[1024,128]{1,0:T(8,128)S(1)} %get-tuple-element.141), kind=kOutput, calls=%fused_computation.2.clone.1 | convolution fusion | flops 805306368 | bytes 2883588 | tf_op jit(solution)/shard_map/while/body/eval_jaxpr/dot_general | solution.py:81
  79.9 2.4 copy.72
  82.3 7.4 %fusion.73 = f32[8,8,64,128]{3,2,1,0:T(8,128)} fusion(f32[8,8,64,128]{3,2,1,0:T(8,128)} %get-tuple-element.127, s32[]{:T(128)S(6)} %copy.77, f32[8,64,1024]{1,2,0:T(8,128)S(1)} %bitcast.81, f32[1024,128]{1,0:T(8,128)S(1)} %get-tuple-element.141), kind=kOutput, calls=%fused_computation.2.clone.1 | convolution fusion | flops 805306368 | bytes 2883588 | tf_op jit(solution)/shard_map/while/body/eval_jaxpr/dot_general | solution.py:81
  94.0 7.4 %fusion.73 = f32[8,8,64,128]{3,2,1,0:T(8,128)} fusion(f32[8,8,64,128]{3,2,1,0:T(8,128)} %get-tuple-element.127, s32[]{:T(128)S(6)} %copy.77, f32[8,64,1024]{1,2,0:T(8,128)S(1)} %bitcast.81, f32[1024,128]{1,0:T(8,128)S(1)} %get-tuple-element.141), kind=kOutput, calls=%fused_computation.2.clone.1 | convolution fusion | flops 805306368 | bytes 2883588 | tf_op jit(solution)/shard_map/while/body/eval_jaxpr/dot_general | solution.py:81
  105.8 7.4 %fusion.73 = f32[8,8,64,128]{3,2,1,0:T(8,128)} fusion(f32[8,8,64,128]{3,2,1,0:T(8,128)} %get-tuple-element.127, s32[]{:T(128)S(6)} %copy.77, f32[8,64,1024]{1,2,0:T(8,128)S(1)} %bitcast.81, f32[1024,128]{1,0:T(8,128)S(1)} %get-tuple-element.141), kind=kOutput, calls=%fused_computation.2.clone.1 | convolution fusion | flops 805306368 | bytes 2883588 | tf_op jit(solution)/shard_map/while/body/eval_jaxpr/dot_general | solution.py:81
  117.5 7.4 %fusion.73 = f32[8,8,64,128]{3,2,1,0:T(8,128)} fusion(f32[8,8,64,128]{3,2,1,0:T(8,128)} %get-tuple-element.127, s32[]{:T(128)S(6)} %copy.77, f32[8,64,1024]{1,2,0:T(8,128)S(1)} %bitcast.81, f32[1024,128]{1,0:T(8,128)S(1)} %get-tuple-element.141), kind=kOutput, calls=%fused_computation.2.clone.1 | convolution fusion | flops 805306368 | bytes 2883588 | tf_op jit(solution)/shard_map/while/body/eval_jaxpr/dot_general | solution.py:81
  129.3 7.4 %fusion.73 = f32[8,8,64,128]{3,2,1,0:T(8,128)} fusion(f32[8,8,64,128]{3,2,1,0:T(8,128)} %get-tuple-element.127, s32[]{:T(128)S(6)} %copy.77, f32[8,64,1024]{1,2,0:T(8,128)S(1)} %bitcast.81, f32[1024,128]{1,0:T(8,128)S(1)} %get-tuple-element.141), kind=kOutput, calls=%fused_computation.2.clone.1 | convolution fusion | flops 805306368 | bytes 2883588 | tf_op jit(solution)/shard_map/while/body/eval_jaxpr/dot_general | solution.py:81
  141.0 7.4 %fusion.73 = f32[8,8,64,128]{3,2,1,0:T(8,128)} fusion(f32[8,8,64,128]{3,2,1,0:T(8,128)} %get-tuple-element.127, s32[]{:T(128)S(6)} %copy.77, f32[8,64,1024]{1,2,0:T(8,128)S(1)} %bitcast.81, f32[1024,128]{1,0:T(8,128)S(1)} %get-tuple-element.141), kind=kOutput, calls=%fused_computation.2.clone.1 | convolution fusion | flops 805306368 | bytes 2883588 | tf_op jit(solution)/shard_map/while/body/eval_jaxpr/dot_general | solution.py:81
  152.8 7.4 %fusion.73 = f32[8,8,64,128]{3,2,1,0:T(8,128)} fusion(f32[8,8,64,128]{3,2,1,0:T(8,128)} %get-tuple-element.127, s32[]{:T(128)S(6)} %copy.77, f32[8,64,1024]{1,2,0:T(8,128)S(1)} %bitcast.81, f32[1024,128]{1,0:T(8,128)S(1)} %get-tuple-element.141), kind=kOutput, calls=%fused_computation.2.clone.1 | convolution fusion | flops 805306368 | bytes 2883588 | tf_op jit(solution)/shard_map/while/body/eval_jaxpr/dot_general | solution.py:81
  160.9 2.8 copy.53
  163.7 2.4 constant_dynamic-slice_fusion
  167.2 2.4 convolution_bitcast_fusion.2
  170.5 87.3 %all-reduce.3.cloned.1.call-done = f32[64,64,128]{2,1,0:T(8,128)} async-done(((f32[64,64,128]{2,1,0:T(8,128)}), f32[64,64,128]{2,1,0:T(8,128)}) %all-reduce.3.cloned.1.call-update) | async-done | bytes 2097168 | tf_op jit(solution)/shard_map/psum | solution.py:89
  257.8 2.5 convert_reduce_fusion
  261.7 6.0 %fusion.57 = (f32[64,8]{1,0:T(8,128)}, f32[64,64,8]{1,2,0:T(8,128)S(1)}) fusion(f32[128,8]{0,1:T(8,128)S(1)} %copy-done.15, bf16[64,64,128]{2,1,0:T(8,128)(2,1)S(1)} %get-tuple-element.71, f32[64,64]{1,0:T(8,128)S(1)} %add_rsqrt_fusion, f32[64,64]{1,0:T(8,128)S(1)} %broadcast_multiply_fusion.2, pred[64]{0:T(512)(128)(4,1)S(1)} %get-tuple-element.68), kind=kOutput, calls=%fused_computation.83 | convolution fusion | flops 51969536 | bytes 1218624 | tf_op jit(solution)/shard_map/dot_general | solution.py:92
  267.7 13.0 %pmax.7 = f32[64,8]{1,0:T(8,128)} all-reduce(f32[64,8]{1,0:T(8,128)} %get-tuple-element.74), channel_id=1, replica_groups=mesh['seq'=16,'row'=4,'col'=4] {'col'}, use_global_device_ids=true, to_apply=%region_8.9 | all-reduce | flops 512 | bytes 4096 | tf_op jit(solution)/shard_map/pmax | solution.py:98
  282.3 11.4 %psum.29 = f32[64,8]{1,0:T(8,128)} all-reduce(f32[64,8]{1,0:T(8,128)} %fusion.42), channel_id=1, replica_groups=mesh['seq'=16,'row'=4,'col'=4] {'col'}, use_global_device_ids=true, to_apply=%region_10.11 | all-reduce | flops 512 | bytes 4096 | tf_op jit(solution)/shard_map/psum | solution.py:100
  293.6 59.5 %all-reduce.5.cloned.1.call-done = bf16[64,64,8]{1,2,0:T(8,128)(2,1)} async-done(((bf16[64,64,8]{1,2,0:T(8,128)(2,1)}), bf16[64,64,8]{1,2,0:T(8,128)(2,1)}) %all-reduce.5.cloned.1.call-update) | async-done | bytes 65552 | tf_op jit(solution)/shard_map/psum | solution.py:126
  357.9 12.8 %psum.31 = f32[64,8]{1,0:T(8,128)S(1)} all-reduce(f32[64,8]{1,0:T(8,128)} %get-tuple-element.72), channel_id=1, replica_groups=mesh['seq'=16,'row'=4,'col'=4] {'col'}, use_global_device_ids=true, to_apply=%region_14.15 | all-reduce | flops 512 | bytes 4096 | tf_op jit(solution)/shard_map/psum | solution.py:127
  370.7 7.2 %fusion.56 = (f32[64,64]{1,0:T(8,128)S(1)}, f32[64,64]{1,0:T(8,128)S(1)}, f32[64,64,128]{2,1,0:T(8,128)S(1)}) fusion(f32[64,64]{1,0:T(8,128)} %copy-done.8, f32[64,64]{1,0:T(8,128)} %copy-done.6, bf16[64,64,128]{2,1,0:T(8,128)(2,1)S(1)} %get-tuple-element.71, f32[128,8]{0,1:T(8,128)S(1)} %copy-done.15, bf16[64,64,8]{1,2,0:T(8,128)(2,1)} %all-reduce.5.cloned.1.call-done, ...), kind=kOutput, calls=%fused_computation.82 | convolution fusion | flops 53665792 | bytes 3418368 | tf_op jit(solution)/shard_map/dot_general | solution.py:129
  378.1 3.3 fusion.15
  (97 shorter events, 50.9 us)
Async XLA Ops:
  7.2 8.2 %copy-start = (bf16[32,16,64]{2,1,0:T(8,128)(2,1)S(1)}, bf16[32,16,64]{2,1,0:T(8,128)(2,1)}, u32[]{:S(2)}) copy-start(bf16[32,16,64]{2,1,0:T(8,128)(2,1)} %param.23) | copy-start | bytes 196612
  7.2 7.1 %copy-start.14 = (bf16[64,256]{1,0:T(8,128)(2,1)S(1)}, bf16[64,256]{1,0:T(8,128)(2,1)}, u32[]{:S(2)}) copy-start(bf16[64,256]{1,0:T(8,128)(2,1)} %param.19) | copy-start | bytes 98308
  7.2 57.5 %all-gather.3.cloned.1.call-start = ((), (), s32[]{:S(2)}) async-start(), calls=%async_computation.1 | async-start | bytes 6684672 | tf_op jit(solution)/shard_map/all_gather | solution.py:65
  10.6 4.8 %copy-start.10 = (bf16[256,64]{0,1:T(8,128)(2,1)S(1)}, bf16[256,64]{0,1:T(8,128)(2,1)}, u32[]{:S(2)}) copy-start(bf16[256,64]{0,1:T(8,128)(2,1)} %param.22) | copy-start | bytes 98308
  14.2 2.2 copy-start.12
  14.2 146.7 %all-gather.5.cloned.1.call-start = ((), (), s32[]{:S(2)}) async-start(), calls=%async_computation.4 | async-start | bytes 1310720 | tf_op jit(solution)/shard_map/all_gather | solution.py:119
  14.6 0.8 copy-start.4
  15.4 50.8 %copy-start.1 = (f32[1024,128]{1,0:T(8,128)S(1)}, f32[1024,128]{1,0:T(8,128)}, u32[]{:S(2)}) copy-start(f32[1024,128]{1,0:T(8,128)} %param.20) | copy-start | bytes 1572868
  16.3 241.5 %all-reduce.3.cloned.1.call-start = ((), (), s32[]{:S(2)}) async-start(), calls=%async_computation.2 | async-start | bytes 4194304 | tf_op jit(solution)/shard_map/psum | solution.py:89
  160.2 0.7 copy-start.13
  160.2 192.9 %all-reduce.5.cloned.1.call-start = ((), (), s32[]{:S(2)}) async-start(), calls=%async_computation.5 | async-start | bytes 262144 | tf_op jit(solution)/shard_map/psum | solution.py:126
  170.4 91.3 %copy-start.15 = (f32[128,8]{0,1:T(8,128)S(1)}, f32[128,8]{0,1:T(8,128)}, u32[]{:S(2)}) copy-start(f32[128,8]{0,1:T(8,128)} %param.21) | copy-start | bytes 12292
  170.4 211.8 %reduce-scatter.2.cloned.1.call-start = ((), (), s32[]{:S(2)}) async-start(), calls=%async_computation.3 | async-start | bytes 1310720 | tf_op jit(solution)/shard_map/reduce_scatter | solution.py:107
  260.3 117.7 %copy-start.2 = (bf16[64,64,128]{2,1,0:T(8,128)(2,1)}, bf16[64,64,128]{2,1,0:T(8,128)(2,1)S(1)}, u32[]{:S(2)}) copy-start(bf16[64,64,128]{2,1,0:T(8,128)(2,1)S(1)} %get-tuple-element.71) | copy-start | bytes 3145732
  260.3 1.4 copy-start.6
  261.7 6.0 %copy-start.8 = (f32[64,64]{1,0:T(8,128)}, f32[64,64]{1,0:T(8,128)S(1)}, u32[]{:S(2)}) copy-start(f32[64,64]{1,0:T(8,128)S(1)} %add_rsqrt_fusion) | copy-start | bytes 49156
  370.7 7.3 %copy-start.7 = (f32[64,64]{1,0:T(8,128)S(1)}, f32[64,64]{1,0:T(8,128)}, u32[]{:S(2)}) copy-start(f32[64,64]{1,0:T(8,128)} %copy-done.6) | copy-start | bytes 49156
  370.7 7.3 %copy-start.9 = (f32[64,64]{1,0:T(8,128)S(1)}, f32[64,64]{1,0:T(8,128)}, u32[]{:S(2)}) copy-start(f32[64,64]{1,0:T(8,128)} %copy-done.8) | copy-start | bytes 49156
  378.0 4.2 %copy-start.3 = (bf16[32,16,64]{2,1,0:T(8,128)(2,1)S(1)}, bf16[32,16,64]{2,1,0:T(8,128)(2,1)}, u32[]{:S(2)}) copy-start(bf16[32,16,64]{2,1,0:T(8,128)(2,1)} %param.13) | copy-start | bytes 196612
  378.0 4.2 %copy-start.5 = (f32[32,16,256]{2,1,0:T(8,128)S(1)}, f32[32,16,256]{2,1,0:T(8,128)}, u32[]{:S(2)}) copy-start(f32[32,16,256]{2,1,0:T(8,128)} %copy-done.4) | copy-start | bytes 1572868
  378.0 4.2 %copy-start.11 = (bf16[256,64]{0,1:T(8,128)(2,1)S(1)}, bf16[256,64]{0,1:T(8,128)(2,1)}, u32[]{:S(2)}) copy-start(bf16[256,64]{0,1:T(8,128)(2,1)} %param.22) | copy-start | bytes 98308
Sparse Core Ops, SparseCore 0:
  14.3 50.2 all-gather.2
  67.0 21.9 all-gather.4
  160.3 97.4 all-reduce.2
  261.8 91.3 all-reduce.4
  358.0 24.1 reduce-scatter.1
where the time goes:
time: 391 us
  waiting for transfers between devices  186 us (48%)
  matrix products  86.3 us (22%)
  blocking collectives  46.8 us (12%)
  local copies, waits for them, and re-layouts  35.7 us (9%)
  other arithmetic  15.6 us (4%)
  between operations  14.2 us (4%)
  loops' own time  5.34 us (1%)
    psum x1, waiting for transfers between devices, on_device(): lax.psum(pieces.reshape(tile_i, tile_j, outer_matrix.shape[1]), 'seq')  87.3 us
    psum x1, waiting for transfers between devices, on_device(): lax.psum(weight_part.astype(jnp.bfloat16), 'seq').astype(jnp.float32)  59.5 us
    dot_general x8, matrix products, one_block(): jnp.dot(outer_rows(0 + number * block_rows, block_rows), outer_matrix, pr...  59.1 us
    all_gather x1, waiting for transfers between devices, on_device(): every_joined = lax.all_gather(joined, ('row', 'col'), axis=1, tiled=True)  38.5 us
    transpose x8, local copies, waits for them, and re-layouts, outer_rows(): jnp.einsum('sic,sjd->ijcd', rows_part, cols_right, preferred_element_type...  19 us
    pmax x1, blocking collectives, on_device(): row_max = lax.pmax(local_peak, 'col')  13 us
    psum x1, blocking collectives, on_device(): inner_sum = lax.psum(jnp.sum(probabilities * grad_weights, axis=1), 'col')  12.8 us
    psum x1, blocking collectives, on_device(): row_sum = lax.psum(jnp.sum(scaled, axis=1), 'col')  11.4 us
  transfers between devices with their start and end apart: 5, of which 4 were waited for; matrix products, arithmetic and copies ran while one was open for 31% of the time, Pallas kernels for 0%

commit v1 on v0

v1 whole, which is shorter than its diff:
```python
import jax
import jax.numpy as jnp
from jax import lax
from jax.experimental import pallas as pl
from jax.experimental.pallas import tpu as pltpu
from jax.sharding import PartitionSpec as P

F32 = jnp.float32
BF16 = jnp.bfloat16
I32 = jnp.int32
EPS = 1e-05
LOW = -1e30
MESH = pl.DeviceIdType.MESH

N = 16
NC = 4
TOK = 16
SEQ = 32
HEADS = 8
FEAT = 64

PAIR_IN, LEFT, RIGHT, VALUES, GRADS, LOGITS, PAIR_OUT, GW, WEIGHTS, GW_SUM, AVG, GW_ALL, GL = range(13)
PHASES = 13


def iota(shape, dim):
    return lax.broadcasted_iota(I32, shape, dim)


def matmul(a, b):
    return jnp.dot(a, b, preferred_element_type=F32)


def matmul_nt(a, b):
    return lax.dot_general(a, b, (((1,), (1,)), ((), ())), preferred_element_type=F32)


def matmul_tn(a, b):
    return lax.dot_general(a, b, (((0,), (0,)), ((), ())), preferred_element_type=F32)


def split(a):
    high = a.astype(BF16)
    return high, (a - high.astype(F32)).astype(BF16)


def normalize(a):
    center = a - jnp.mean(a, axis=-1, keepdims=True)
    inverse = lax.rsqrt(jnp.mean(center * center, axis=-1, keepdims=True) + EPS)
    return center * inverse, inverse


def swap_blocks(arrays, width):
    arrays = list(arrays)
    lanes = arrays[0].shape[1]
    block = iota(arrays[0].shape, 1) // width
    bit = len(arrays) // 2
    while bit:
        upper = (block & bit) != 0
        for low in range(len(arrays)):
            if low & bit:
                continue
            a, b = arrays[low], arrays[low | bit]
            arrays[low] = jnp.where(upper, pltpu.roll(b, bit * width, 1), a)
            arrays[low | bit] = jnp.where(upper, b, pltpu.roll(a, lanes - bit * width, 1))
        bit //= 2
    return arrays


def kernel(
    mask_s, mask_v, x_ref, adj_ref, w1_ref, w2_ref, wc_ref, ws_ref, wf_ref, score_ref, m_hbm, pair_hbm,
    out_al, out_pair, out_grad,
    xn_scr, lbuf, rbuf, l_all, r_all, vbuf, gbuf, vh, gh, gate_scr, wf_blk, m_scr, m_hl,
    pin_tile, pin_scr, o_scr, p_scr, po_scr, po_tile, po_all, lg_src, lg_all, prob_scr, wbuf, wh,
    avbuf, avrx, gwbuf, gwrx, rsbuf, rsrx, agbuf, agrx, glbuf, glrx, gl_scr,
    send_sem, recv_sem, local_sem,
):
    S = lax.axis_index("seq")
    row = lax.axis_index("row")
    col = lax.axis_index("col")
    T = row * NC + col
    y = S // NC
    xpos = S % NC

    def device(s, t):
        return (s, t // NC, t % NC)

    def remote(src, dst, phase, s, t):
        return pltpu.make_async_remote_copy(
            src_ref=src, dst_ref=dst, send_sem=send_sem.at[phase], recv_sem=recv_sem.at[phase],
            device_id=device(s, t), device_id_type=MESH,
        )

    def local(src, dst, phase):
        pltpu.make_async_copy(src, dst, recv_sem.at[phase]).start()

    def wait_recv(buf, phase):
        pltpu.make_async_copy(buf, buf, recv_sem.at[phase]).wait()

    def wait_send(buf, phase):
        pltpu.make_async_copy(buf, buf, send_sem.at[phase]).wait()

    barrier = pltpu.get_barrier_semaphore()

    def greet(s, t):
        pl.semaphore_signal(barrier, inc=1, device_id=device(s, t), device_id_type=MESH)

    @pl.loop(1, N)
    def _(d):
        greet((S + d) % N, T)
        greet(S, (T + d) % N)
        greet((S + d) % N, S)

    @pl.when(S != T)
    def _():
        greet(S, S)

    @pl.loop(0, N)
    def _(e):
        s, t = col * NC + e // NC, row * NC + e % NC

        @pl.when(jnp.logical_or(s != S, t != T))
        def _():
            greet(s, t)

    m_copy = pltpu.make_async_copy(m_hbm, m_scr, local_sem.at[0])
    m_copy.start()

    xn = normalize(x_ref[...].reshape(SEQ * TOK, FEAT).astype(F32))[0].astype(BF16).astype(F32)
    xn_scr[...] = xn

    lane = iota((32, 256), 1)
    chan = iota((32, 256), 0)
    same = lane % 32 == chan
    pick_left = jnp.where(jnp.logical_and(same, lane < 128), 1.0, 0.0).astype(BF16)
    pick_right = jnp.where(jnp.logical_and(same, lane >= 128), 1.0, 0.0).astype(BF16)
    both = matmul(w1_ref[...], pick_left) + matmul(w2_ref[...], pick_right)
    quarter = (iota((FEAT, 256), 1) // 32) % 4
    w_lr = jnp.concatenate([jnp.where(quarter == q, both, 0.0) for q in range(4)], axis=0).astype(BF16)
    x_lr = []
    for q in range(4):
        parts = []
        for group in range(4):
            token = 4 * group + q
            parts.append(
                xn_scr[pl.ds(token, SEQ, stride=TOK), :] * mask_s[T * TOK + token].astype(F32)
            )
        x_lr.append(jnp.concatenate(parts, axis=0))
    factors = matmul(jnp.concatenate(x_lr, axis=1).astype(BF16), w_lr).astype(BF16)
    lbuf[...] = factors[:, :128].reshape(4, SEQ, 128)
    rbuf[...] = factors[:, 128:].reshape(4, SEQ, 128)

    pl.semaphore_wait(
        barrier,
        4 * N - 2 - jnp.where(S == T, 1, 0).astype(I32) - jnp.where(y == col, 1, 0).astype(I32),
    )

    my_tile = pair_hbm.at[pl.ds(col * TOK, TOK), pl.ds(xpos * TOK, TOK), :]

    @pl.when(y == col)
    def _():
        local(my_tile, pin_tile, PAIR_IN)

        @pl.loop(1, NC)
        def _(d):
            c = (col + d) % NC
            remote(
                pair_hbm.at[pl.ds(c * TOK, TOK), pl.ds(xpos * TOK, TOK), :], pin_tile, PAIR_IN, S, row * NC + c
            ).start()

    mine = pl.ds(S * SEQ, SEQ)
    local(lbuf, l_all.at[:, mine, :], LEFT)

    @pl.when(S == T)
    def _():
        local(rbuf, r_all.at[:, mine, :], RIGHT)

    @pl.when(S != T)
    def _():
        remote(rbuf, r_all.at[:, mine, :], RIGHT, T, T).start()

    @pl.loop(1, N)
    def _(d):
        remote(lbuf, l_all.at[:, mine, :], LEFT, (S + d) % N, T).start()
        remote(rbuf, r_all.at[:, mine, :], RIGHT, T, (T + d) % N).start()

    lane = iota((256, 1024), 1)
    chan = iota((256, 1024), 0)
    pick = jnp.where(
        jnp.logical_and(lane // 128 == chan // 32, lane % 32 == chan % 32), 1.0, 0.0
    ).astype(BF16)
    quarter = (iota((FEAT, 1024), 1) // 32) % 4

    def spread(w):
        return jnp.concatenate([jnp.where(quarter == q, w, 0.0) for q in range(4)], axis=0).astype(BF16)

    def by_group(a):
        a = a.reshape(8, 4, TOK, FEAT)
        return jnp.concatenate([a[:, q].reshape(8 * TOK, FEAT) for q in range(4)], axis=1)

    def to_pieces(a, buf):
        for h in range(HEADS):
            buf[2 * h : 2 * h + 2] = a[:, h * 128 : (h + 1) * 128].reshape(2, 4, TOK, 128)

    tokens = pl.ds(T * TOK, TOK)

    def send_column(buf, dst, phase):
        local(buf.at[T], dst, phase)

        @pl.loop(1, N)
        def _(d):
            t = (T + d) % N
            remote(buf.at[t], dst, phase, S, t).start()

    x_v = by_group(xn).astype(BF16)
    to_pieces(matmul(x_v, spread(matmul(wc_ref[...], pick))).astype(BF16), vbuf)
    send_column(vbuf, vh.at[:, tokens, :], VALUES)
    gate = jax.nn.sigmoid(matmul(x_v, spread(matmul(ws_ref[...], pick))))
    gate_scr[...] = gate
    wf_blk[...] = spread(matmul_tn(wf_ref[...], pick))
    x_g = by_group(adj_ref[...].astype(F32)).astype(BF16)
    to_pieces((matmul(x_g, wf_blk[...]) * gate).astype(BF16), gbuf)
    send_column(gbuf, gh.at[:, tokens, :], GRADS)

    m_copy.wait()
    m_high, m_low = split(m_scr[...])
    m_hl[:, :128] = m_high
    m_hl[:, 128:] = m_low
    score = score_ref[...]
    repeat = jnp.where(iota((HEADS, 128), 1) // TOK == iota((HEADS, 128), 0), 1.0, 0.0).astype(BF16)

    def repeated(a):
        high, low = split(a)
        return matmul(high, repeat).astype(BF16), matmul(low, repeat).astype(BF16)

    score_high, score_low = repeated(score)
    wait_recv(pin_tile, PAIR_IN)
    pin_scr[...] = pin_tile[...].reshape(TOK * TOK, 128).astype(F32)

    wait_recv(l_all, LEFT)
    wait_recv(r_all, RIGHT)
    left = jnp.concatenate([l_all[g] for g in range(4)], axis=1)
    right = jnp.concatenate([r_all[g] for g in range(4)], axis=1)
    outer = matmul_tn(left, right)
    for g in range(4):
        o_scr[g] = outer[:, g * 128 : (g + 1) * 128]

    @pl.loop(0, 8)
    def _(cg):
        parts = [
            jnp.concatenate([o_scr[g, pl.ds(4 * cg + q, TOK, stride=32), :] for g in range(4)], axis=0)
            for q in range(4)
        ]
        parts = swap_blocks(parts, 32)
        lanes = pl.ds(pl.multiple_of(cg * 128, 128), 128)
        for j in range(TOK):
            p_scr[pl.ds(j * TOK, TOK), lanes] = parts[j % 4][(j // 4) * TOK : (j // 4 + 1) * TOK]

    p_high, p_low = split(p_scr[...])
    product = matmul(p_high, m_hl[...])
    update = product[:, :128] + (product[:, 128:] + matmul(p_low, m_hl[:, :128]))
    pin = jnp.concatenate([pin_scr[pl.ds(j, TOK, stride=TOK), :] for j in range(TOK)], axis=0)
    pair_tile = (pin + update).astype(BF16).astype(F32)
    normal = normalize(pair_tile)[0]
    n_high, n_low = split(normal)
    logits = matmul(n_high, score_high) + (matmul(n_high, score_low) + matmul(n_low, score_high))
    own = iota((TOK, 1, 128), 2) % TOK == iota((TOK, 1, 128), 0)
    lg_src[...] = jnp.sum(jnp.where(own, logits.reshape(TOK, TOK, 128), 0.0), axis=0)

    def send_plane(src, dst, phase):
        local(src, dst, phase)

        @pl.loop(1, N)
        def _(d):
            remote(src, dst, phase, (S + d) % N, T).start()

    send_plane(lg_src, lg_all.at[S], LOGITS)
    po_scr[...] = pair_tile
    for i in range(TOK):
        po_tile[i] = po_scr[pl.ds(i, TOK, stride=TOK), :].astype(BF16)
    place = po_all.at[pl.ds(col * TOK, TOK), pl.ds(xpos * TOK, TOK), :]
    owner = row * NC + y

    @pl.when(y == col)
    def _():
        local(po_tile, place, PAIR_OUT)

    @pl.when(y != col)
    def _():
        remote(po_tile, place, PAIR_OUT, S, owner).start()

    @pl.loop(1, N)
    def _(d):
        remote(po_tile, place, PAIR_OUT, (S + d) % N, owner).start()

    wait_recv(vh, VALUES)
    wait_recv(gh, GRADS)
    v_cat = jnp.concatenate([vh[g] for g in range(4)], axis=1)
    g_cat = jnp.concatenate([gh[g] for g in range(4)], axis=1)
    gwbuf[...] = matmul_nt(g_cat, v_cat).astype(BF16).reshape(N, TOK, 256)
    send_column(gwbuf, gwrx.at[T], GW)

    wait_recv(lg_all, LOGITS)
    lg = lg_all[...].reshape(2, 8, TOK, 128)
    parts = swap_blocks([lg[:, s].reshape(2 * TOK, 128) for s in range(8)], TOK)
    lg = jnp.stack([jnp.concatenate([a[:TOK], a[TOK:]], axis=1) for a in parts], axis=0)
    maskf = mask_v[...].astype(F32).reshape(1, 1, 256)
    lg = jnp.where(maskf > 0, lg, LOW)
    scaled = jnp.exp(lg - jnp.max(lg, axis=-1, keepdims=True)) * maskf
    prob = scaled / jnp.sum(scaled, axis=-1, keepdims=True)
    prob_scr[...] = prob
    wbuf[...] = prob.astype(BF16)
    local(wbuf.at[T // 2], wh.at[tokens, :], WEIGHTS)

    @pl.loop(1, N)
    def _(d):
        t = (T + d) % N
        remote(wbuf.at[t // 2], wh.at[tokens, :], WEIGHTS, S, t).start()

    wait_recv(gwrx, GW)
    gw = gwrx[...].astype(F32).reshape(HEADS, 2, TOK, 256)
    gw = (gw[:, 0] + gw[:, 1]).astype(BF16)
    for h in range(HEADS):
        rsbuf[2 * h] = gw[h, :, :128]
        rsbuf[2 * h + 1] = gw[h, :, 128:]
    local(rsbuf.at[S], rsrx.at[S], GW_SUM)

    @pl.loop(1, N)
    def _(d):
        s = (S + d) % N
        remote(rsbuf.at[s], rsrx.at[S], GW_SUM, s, T).start()

    wait_recv(wh, WEIGHTS)
    avg = matmul(wh[...], v_cat).astype(BF16)
    for g in range(4):
        avbuf[:, g] = avg[:, g * 128 : (g + 1) * 128].reshape(N, TOK, 128)
    send_column(avbuf, avrx.at[T], AVG)

    wait_recv(rsrx, GW_SUM)
    agbuf[...] = jnp.sum(rsrx[...].astype(F32), axis=0).astype(BF16)
    send_plane(agbuf, agrx.at[S], GW_ALL)

    wait_recv(agrx, GW_ALL)
    gw = agrx[...].astype(F32).reshape(HEADS, 2, TOK, 128)
    gw = jnp.concatenate([gw[:, 0], gw[:, 1]], axis=-1)
    prob = prob_scr[...]
    gl = prob * (gw - jnp.sum(prob * gw, axis=-1, keepdims=True))
    parts = [jnp.concatenate([gl[h, :, :128], gl[h, :, 128:]], axis=0) for h in range(HEADS)]
    parts = swap_blocks(parts, TOK)
    for s in range(8):
        glbuf[s // 4, s % 4] = parts[s][:TOK].astype(BF16)
        glbuf[2 + s // 4, s % 4] = parts[s][TOK:].astype(BF16)
    local(glbuf.at[col], glrx.at[col], GL)

    @pl.loop(1, NC)
    def _(d):
        c = (col + d) % NC
        remote(glbuf.at[c], glrx.at[col], GL, S, row * NC + c).start()

    wait_recv(avrx, AVG)
    gated = jnp.concatenate(
        [avrx[2 * h : 2 * h + 2].reshape(8 * TOK, 128).astype(F32) for h in range(HEADS)], axis=1
    )
    gated = (gated * gate_scr[...]).astype(BF16)
    mixed = matmul_nt(gated, wf_blk[...])
    result = (by_group(x_ref[...].astype(F32)) + mixed).astype(BF16)
    for q in range(4):
        out_al[:, q] = result[:, q * FEAT : (q + 1) * FEAT].reshape(8, TOK, FEAT)

    wait_recv(po_all, PAIR_OUT)
    po_copy = pltpu.make_async_copy(po_all, out_pair, local_sem.at[1])
    po_copy.start()
    center = score - jnp.mean(score, axis=0, keepdims=True)
    c_high, c_low = repeated(center)
    c_hl = jnp.concatenate([c_high, c_low], axis=0)
    own = (iota((1, 1, TOK, 128), 3) % TOK) == iota((1, 1, TOK, 128), 2)
    wait_recv(glrx, GL)
    for c in range(NC):
        for s in range(NC):
            gl_scr[pl.ds(c * TOK, TOK), s] = glrx[c, s].astype(F32).reshape(TOK, 1, 128)
    rows_at_once = 8

    @pl.loop(0, 64 // rows_at_once)
    def _(b):
        rows = pl.ds(b * rows_at_once, rows_at_once)
        block = po_all[rows].reshape(rows_at_once * 64, 128).astype(F32)
        normal, inverse = normalize(block)
        spread_gl = jnp.where(own, gl_scr[rows], 0.0)
        spread_gl = spread_gl.astype(BF16).reshape(rows_at_once * 64, 128)
        grad = matmul_nt(spread_gl, c_hl)
        grad = grad[:, :128] + grad[:, 128:]
        along = jnp.mean(grad * normal, axis=-1, keepdims=True)
        out_grad[rows] = (inverse * (grad - normal * along)).astype(BF16).reshape(rows_at_once, 64, 128)

    po_copy.wait()

    @pl.when(y == col)
    def _():
        third = pair_hbm.at[pl.ds(0, 3 * TOK), pl.ds(0, TOK), :]
        wait_send(third, PAIR_IN)
        wait_send(po_all.at[pl.ds(0, 60)], PAIR_OUT)

    @pl.when(y != col)
    def _():
        wait_send(po_all, PAIR_OUT)

    wait_send(l_all.at[:, pl.ds(0, 15 * SEQ), :], LEFT)

    @pl.when(S == T)
    def _():
        wait_send(r_all.at[:, pl.ds(0, 15 * SEQ), :], RIGHT)

    @pl.when(S != T)
    def _():
        wait_send(r_all, RIGHT)

    wait_send(vh.at[:, pl.ds(0, 15 * TOK), :], VALUES)
    wait_send(gh.at[:, pl.ds(0, 15 * TOK), :], GRADS)
    wait_send(lg_all.at[pl.ds(0, 15)], LOGITS)
    wait_send(gwrx.at[pl.ds(0, 15)], GW)
    wait_send(wh.at[pl.ds(0, 15 * TOK), :], WEIGHTS)
    wait_send(rsrx.at[pl.ds(0, 15)], GW_SUM)
    wait_send(avrx.at[pl.ds(0, 15)], AVG)
    wait_send(agrx.at[pl.ds(0, 15)], GW_ALL)
    wait_send(glrx.at[pl.ds(0, 3)], GL)


def on_device(
    alignment_input,
    pair_input,
    token_valid_mask,
    first_factor_weights,
    second_factor_weights,
    content_weights_grid,
    sigmoid_weights_grid,
    outer_matrix,
    score_matrix,
    final_mixing_weights,
    adjoint_of_rowset,
):
    vmem = pl.BlockSpec(memory_space=pltpu.VMEM)
    smem = pl.BlockSpec(memory_space=pltpu.SMEM)
    anywhere = pl.BlockSpec(memory_space=pl.ANY)
    V = pltpu.VMEM
    scratch = [
        V((SEQ * TOK, FEAT), F32),
        V((4, SEQ, 128), BF16),
        V((4, SEQ, 128), BF16),
        V((4, N * SEQ, 128), BF16),
        V((4, N * SEQ, 128), BF16),
        V((N, 4, TOK, 128), BF16),
        V((N, 4, TOK, 128), BF16),
        V((4, 256, 128), BF16),
        V((4, 256, 128), BF16),
        V((128, 1024), F32),
        V((256, 1024), BF16),
        V((1024, 128), F32),
        V((1024, 256), BF16),
        V((TOK, TOK, 128), BF16),
        V((TOK * TOK, 128), F32),
        V((4, 512, 128), F32),
        V((256, 1024), F32),
        V((256, 128), F32),
        V((TOK, TOK, 128), BF16),
        V((64, 64, 128), BF16),
        V((TOK, 128), F32),
        V((N, TOK, 128), F32),
        V((HEADS, TOK, 256), F32),
        V((HEADS, TOK, 256), BF16),
        V((256, 256), BF16),
        V((N, 4, TOK, 128), BF16),
        V((N, 4, TOK, 128), BF16),
        V((N, TOK, 256), BF16),
        V((N, TOK, 256), BF16),
        V((N, TOK, 128), BF16),
        V((N, TOK, 128), BF16),
        V((TOK, 128), BF16),
        V((N, TOK, 128), BF16),
        V((NC, NC, TOK, 128), BF16),
        V((NC, NC, TOK, 128), BF16),
        V((64, NC, 1, 128), F32),
        pltpu.SemaphoreType.DMA((PHASES,)),
        pltpu.SemaphoreType.DMA((PHASES,)),
        pltpu.SemaphoreType.DMA((2,)),
    ]
    grouped = (8, 4, TOK, FEAT)
    aligned, pair_output, pair_gradient = pl.pallas_call(
        kernel,
        out_shape=[
            jax.ShapeDtypeStruct(grouped, BF16),
            jax.ShapeDtypeStruct((64, 64, 128), BF16),
            jax.ShapeDtypeStruct((64, 64, 128), BF16),
        ],
        in_specs=[smem] + [vmem] * 9 + [anywhere] * 2,
        out_specs=[vmem, anywhere, vmem],
        scratch_shapes=scratch,
        compiler_params=pltpu.CompilerParams(
            collective_id=0, has_side_effects=True, vmem_limit_bytes=48 * 1024 * 1024
        ),
        name="msa_block",
    )(
        token_valid_mask,
        token_valid_mask.reshape(1, 256),
        alignment_input.reshape(grouped),
        adjoint_of_rowset.reshape(grouped),
        first_factor_weights,
        second_factor_weights,
        content_weights_grid,
        sigmoid_weights_grid,
        final_mixing_weights,
        score_matrix,
        outer_matrix,
        pair_input,
    )
    return aligned.reshape(SEQ, TOK, FEAT), pair_output, pair_gradient


def solution(mesh):
    in_specs = (
        P("seq", ("row", "col"), None),
        P("row", "col", None),
        P(),
        P(),
        P(),
        P(),
        P(),
        P(),
        P(),
        P(),
        P("seq", ("row", "col"), None),
    )
    out_specs = (P("seq", ("row", "col"), None), P("row", "col", None), P("row", "col", None))
    return jax.shard_map(
        on_device, mesh=mesh, in_specs=in_specs, out_specs=out_specs, check_vma=False
    )
```

time: 391 us -> 97.2 us (0.25)
  waiting for transfers between devices: 186 us -> 0 us
  Pallas kernels: 0 us -> 87 us
  matrix products: 86.3 us -> 0 us
  blocking collectives: 46.8 us -> 0 us
  local copies, waits for them, and re-layouts: 35.7 us -> 9.08 us
  other arithmetic: 15.6 us -> 0 us
  between operations: 14.2 us -> 0.71 us
  loops' own time: 5.34 us -> 0 us
    psum x2 -> x0, waiting for transfers between devices: 147 us -> none  [the longest x1 87.3 us: on_device(): lax.psum(pieces.reshape(tile_i, tile_j, outer_matrix.shape[1]), 'seq')]
    pallas_call x0 -> x1, Pallas kernels: none -> 87 us  [on_device(): pl.pallas_call(kernel, out_shape=[jax.ShapeDtypeStruct(grouped, BF16), ja...]
    dot_general x26 -> x0, matrix products: 86.3 us -> none  [the longest x8 59.1 us: one_block(): jnp.dot(outer_rows(0 + number * block_rows, block_rows), outer_matrix, pr...]
    all_gather x2 -> x0, waiting for transfers between devices: 38.5 us -> none  [the longest x1 38.5 us: on_device(): every_joined = lax.all_gather(joined, ('row', 'col'), axis=1, tiled=True)]
    psum x2 -> x0, blocking collectives: 24.2 us -> none  [the longest x1 12.8 us: on_device(): inner_sum = lax.psum(jnp.sum(probabilities * grad_weights, axis=1), 'col')]
    transpose x8 -> x0, local copies, waits for them, and re-layouts: 19 us -> none  [outer_rows(): jnp.einsum('sic,sjd->ijcd', rows_part, cols_right, preferred_element_type...]
    pmax x1 -> x0, blocking collectives: 13 us -> none  [on_device(): row_max = lax.pmax(local_peak, 'col')]
    all_gather x1 -> x0, blocking collectives: 9.57 us -> none  [on_device(): rows_left = lax.all_gather(left_proj, 'col', axis=1, tiled=True)]
  transfers between devices with their start and end apart: 5 -> 0, of which waited for: 4 -> 0; matrix products, arithmetic and copies ran while one was open for 31% -> 0% of each run, Pallas kernels for 0% -> 0%
where the time goes in v1:
time: 97.2 us; the launch traced here: 96.8 us
  Pallas kernels  87 us (90%)
  local copies, waits for them, and re-layouts  9.08 us (9%)
    pallas_call x1, Pallas kernels, on_device(): pl.pallas_call(kernel, out_shape=[jax.ShapeDtypeStruct(grouped, BF16), ja...  87 us
    unnamed x21, local copies, waits for them, and re-layouts  9.08 us

profile of v1, /device:TPU:1, one launch (start us, length us, event | category | flops | bytes accessed | tf_op | source)
XLA Modules:
  0.0 96.8 jit_solution(17872910007888829955)
XLA Ops:
  0.6 0.0 copy-start.2
  0.6 0.8 copy.14.w1_ref
  1.5 0.8 copy.15.w2_ref
  2.3 0.8 copy.17.score_ref
  3.0 0.0 copy-start.4
  3.1 0.0 copy-start.5
  3.1 0.0 copy-start.6
  3.1 0.9 copy.16.wf_ref
  4.0 0.0 copy-done.2
  4.0 0.0 copy-done.4
  4.0 0.0 copy-done.5
  4.0 0.0 copy-done.6
  4.0 0.0 copy-start
  4.0 1.2 %copy-done = bf16[64,64,128]{2,1,0:T(8,128)(2,1)S(1)} copy-done((bf16[64,64,128]{2,1,0:T(8,128)(2,1)S(1)}, bf16[64,64,128]{2,1,0:T(8,128)(2,1)}, u32[]{:S(2)}) %copy-start) | copy-done | bytes 1048600
  5.2 0.0 copy-start.1
  5.2 1.0 %copy-done.1 = f32[1024,128]{1,0:T(8,128)S(1)} copy-done((f32[1024,128]{1,0:T(8,128)S(1)}, f32[1024,128]{1,0:T(8,128)}, u32[]{:S(2)}) %copy-start.1) | copy-done | bytes 524312
  6.3 0.0 copy-start.3
  6.3 0.9 copy-done.3
  7.2 87.0 %msa_block.1 = (bf16[8,4,16,64]{3,2,1,0:T(8,128)(2,1)S(1)}, bf16[64,64,128]{2,1,0:T(8,128)(2,1)S(1)}, bf16[64,64,128]{2,1,0:T(8,128)(2,1)S(1)}) custom-call(s32[256]{0:T(256)S(1)} %copy-done.6, s32[1,256]{1,0:T(1,128)S(1)} %bitcast.7, bf16[8,4,16,64]{3,2,1,0:T(8,128)(2,1)S(1)} %bitcast.4, bf16[8,4,16,64]{3,2,1,0:T(8,128)(2,1)S(1)} %bitcast.5, ...), custom_call_target="tpu_custom_call" | custom-call | tf_op jit(solution)/shard_map/msa_block/pallas_call | solution.py:487
  94.2 0.7 copy.21
  94.9 1.0 %copy.22 = bf16[64,64,128]{2,1,0:T(8,128)(2,1)} copy(bf16[64,64,128]{2,1,0:T(8,128)(2,1)S(1)} %get-tuple-element.13) | data formatting | bytes 2097152
  95.9 1.0 %copy.23 = bf16[64,64,128]{2,1,0:T(8,128)(2,1)} copy(bf16[64,64,128]{2,1,0:T(8,128)(2,1)S(1)} %get-tuple-element.14) | data formatting | bytes 2097152
Async XLA Ops:
  0.6 3.3 %copy-start.2 = (bf16[32,16,64]{2,1,0:T(8,128)(2,1)S(1)}, bf16[32,16,64]{2,1,0:T(8,128)(2,1)}, u32[]{:S(2)}) copy-start(bf16[32,16,64]{2,1,0:T(8,128)(2,1)} %param.11) | copy-start | bytes 196612
  3.0 0.9 copy-start.4
  3.1 0.9 copy-start.5
  3.1 0.9 copy-start.6
  4.0 1.2 %copy-start = (bf16[64,64,128]{2,1,0:T(8,128)(2,1)S(1)}, bf16[64,64,128]{2,1,0:T(8,128)(2,1)}, u32[]{:S(2)}) copy-start(bf16[64,64,128]{2,1,0:T(8,128)(2,1)} %pair_hbm.1) | copy-start | bytes 3145732
  5.2 1.0 %copy-start.1 = (f32[1024,128]{1,0:T(8,128)S(1)}, f32[1024,128]{1,0:T(8,128)}, u32[]{:S(2)}) copy-start(f32[1024,128]{1,0:T(8,128)} %m_hbm.1) | copy-start | bytes 1572868
  6.3 0.9 copy-start.3

commit v2 on v1

v2 whole, which is shorter than its diff:
```python
import jax
import jax.numpy as jnp
from jax import lax
from jax.experimental import pallas as pl
from jax.experimental.pallas import tpu as pltpu
from jax.sharding import PartitionSpec as P

F32 = jnp.float32
BF16 = jnp.bfloat16
I32 = jnp.int32
EPS = 1e-05
LOW = -1e30
MESH = pl.DeviceIdType.MESH

N = 16
NC = 4
TOK = 16
SEQ = 32
HEADS = 8
FEAT = 64

PAIR_IN, LEFT, SWAP, RIGHT, RIGHT_SIB, NORM, NORM_SIB, LOGITS, TURN, PAIR_OUT, GW_SUM, GW_ALL, GL = range(13)
PHASES = 13


def iota(shape, dim):
    return lax.broadcasted_iota(I32, shape, dim)


def matmul(a, b):
    return jnp.dot(a, b, preferred_element_type=F32)


def matmul_nt(a, b):
    return lax.dot_general(a, b, (((1,), (1,)), ((), ())), preferred_element_type=F32)


def matmul_tn(a, b):
    return lax.dot_general(a, b, (((0,), (0,)), ((), ())), preferred_element_type=F32)


def split(a):
    high = a.astype(BF16)
    return high, (a - high.astype(F32)).astype(BF16)


def normalize(a):
    center = a - jnp.mean(a, axis=-1, keepdims=True)
    inverse = lax.rsqrt(jnp.mean(center * center, axis=-1, keepdims=True) + EPS)
    return center * inverse, inverse


def swap_blocks(arrays, width):
    arrays = list(arrays)
    lanes = arrays[0].shape[1]
    block = iota(arrays[0].shape, 1) // width
    bit = len(arrays) // 2
    while bit:
        upper = (block & bit) != 0
        for low in range(len(arrays)):
            if low & bit:
                continue
            a, b = arrays[low], arrays[low | bit]
            arrays[low] = jnp.where(upper, pltpu.roll(b, bit * width, 1), a)
            arrays[low | bit] = jnp.where(upper, b, pltpu.roll(a, lanes - bit * width, 1))
        bit //= 2
    return arrays


def kernel(
    mask_s, x_hbm, adj_hbm, w1_hbm, w2_hbm, wc_hbm, ws_hbm, wf_hbm, score_hbm, m_hbm, pair_hbm,
    out_al, out_pair, out_grad,
    x_ref, adj_ref, w1_ref, w2_ref, wc_ref, ws_ref, wf_ref, score_ref, m_scr,
    xn_scr, lbuf, rbuf, rmid, l_all, r_all, nbuf, nv, vh, gbuf, gate_scr, wc_blk, wf_blk, m_hl,
    pin_tile, pin_scr, o_scr, p_scr, po_scr, po_tile, po_mid, po_all, lg_src, lg_all, prob_scr,
    rsbuf, rsrx, agbuf, agrx, glbuf, glrx, gl_scr,
    send_sem, recv_sem, local_sem,
):
    S = lax.axis_index("seq")
    row = lax.axis_index("row")
    col = lax.axis_index("col")
    T = row * NC + col
    y = S // NC
    xpos = S % NC
    core = T % 2
    sibling = T + 1 - 2 * core

    def slot(n):
        return (n % 2) * (N // 2) + n // 2

    def device(s, t):
        return (s, t // NC, t % NC)

    def remote(src, dst, phase, s, t):
        return pltpu.make_async_remote_copy(
            src_ref=src, dst_ref=dst, send_sem=send_sem.at[phase], recv_sem=recv_sem.at[phase],
            device_id=device(s, t), device_id_type=MESH,
        )

    def local(src, dst, phase):
        pltpu.make_async_copy(src, dst, recv_sem.at[phase]).start()

    def wait_recv(buf, phase):
        pltpu.make_async_copy(buf, buf, recv_sem.at[phase]).wait()

    def wait_send(buf, phase):
        pltpu.make_async_copy(buf, buf, send_sem.at[phase]).wait()

    loads = []
    for n, (src, dst) in enumerate(
        [
            (x_hbm, x_ref), (w1_hbm, w1_ref), (w2_hbm, w2_ref), (wc_hbm, wc_ref), (ws_hbm, ws_ref),
            (wf_hbm, wf_ref), (adj_hbm, adj_ref), (score_hbm, score_ref), (m_hbm, m_scr),
        ]
    ):
        copy = pltpu.make_async_copy(src, dst, local_sem.at[n])
        copy.start()
        loads.append(copy)

    barrier = pltpu.get_barrier_semaphore()

    def greet(s, t):
        pl.semaphore_signal(barrier, inc=1, device_id=device(s, t), device_id_type=MESH)

    @pl.loop(1, N)
    def _(d):
        greet((S + d) % N, T)

    @pl.loop(1, N // 2)
    def _(d):
        greet(S, (T + 2 * d) % N)

    greet(S, sibling)

    @pl.loop(1, NC)
    def _(d):
        greet(S, row * NC + (col + d) % NC)

    @pl.when(S != T)
    def _():
        greet(T, S)

    @pl.when(y != col)
    def _():
        greet(col * NC + xpos, row * NC + y)

    greeted = N - 1 + N // 2 - 1 + 1 + NC - 1
    greeted = greeted + jnp.where(S != T, 1, 0).astype(I32) + jnp.where(y != col, 1, 0).astype(I32)

    loads[0].wait()
    xn = normalize(x_ref[...].reshape(SEQ * TOK, FEAT).astype(F32))[0].astype(BF16).astype(F32)
    xn_scr[...] = xn

    def by_group(a):
        a = a.reshape(8, 4, TOK, FEAT)
        return jnp.concatenate([a[:, q].reshape(8 * TOK, FEAT) for q in range(4)], axis=1)

    x_v = by_group(xn).astype(BF16)
    nbuf[...] = x_v.reshape(8, TOK, 256)

    loads[1].wait()
    loads[2].wait()
    lane = iota((32, 256), 1)
    chan = iota((32, 256), 0)
    same = lane % 32 == chan
    pick_left = jnp.where(jnp.logical_and(same, lane < 128), 1.0, 0.0).astype(BF16)
    pick_right = jnp.where(jnp.logical_and(same, lane >= 128), 1.0, 0.0).astype(BF16)
    both = matmul_tn(w1_ref[...], pick_left) + matmul_tn(w2_ref[...], pick_right)
    quarter = (iota((FEAT, 256), 1) // 32) % 4
    w_lr = jnp.concatenate([jnp.where(quarter == q, both, 0.0) for q in range(4)], axis=0).astype(BF16)
    x_lr = []
    for q in range(4):
        parts = []
        for group in range(4):
            token = 4 * group + q
            parts.append(
                xn_scr[pl.ds(token, SEQ, stride=TOK), :] * mask_s[T * TOK + token].astype(F32)
            )
        x_lr.append(jnp.concatenate(parts, axis=0))
    factors = matmul(jnp.concatenate(x_lr, axis=1).astype(BF16), w_lr).astype(BF16)
    lbuf[...] = factors[:, :128].reshape(4, SEQ, 128)
    rbuf[...] = factors[:, 128:].reshape(4, SEQ, 128)

    pl.semaphore_wait(barrier, greeted)

    @pl.when(S == T)
    def _():
        local(rbuf, rmid, SWAP)

    @pl.when(S != T)
    def _():
        remote(rbuf, rmid, SWAP, T, S).start()

    mine = pl.ds(slot(S) * SEQ, SEQ)
    local(lbuf, l_all.at[:, mine, :], LEFT)

    @pl.loop(1, N)
    def _(d):
        remote(lbuf, l_all.at[:, mine, :], LEFT, (S + d) % N, T).start()

    tokens = pl.ds(slot(T) * TOK, TOK)

    def send_norm(d):
        remote(nbuf, nv.at[:, tokens, :], NORM, S, (T + 2 * d) % N).start()

    local(nbuf, nv.at[:, tokens, :], NORM)
    for d in (1, 7, 2, 6):
        send_norm(d)

    my_tile = pair_hbm.at[pl.ds(col * TOK, TOK), pl.ds(xpos * TOK, TOK), :]

    @pl.when(y == col)
    def _():
        local(my_tile, pin_tile, PAIR_IN)

        @pl.loop(1, NC)
        def _(d):
            c = (col + d) % NC
            remote(
                pair_hbm.at[pl.ds(c * TOK, TOK), pl.ds(xpos * TOK, TOK), :], pin_tile, PAIR_IN, S, row * NC + c
            ).start()

    lane = iota((256, 1024), 1)
    chan = iota((256, 1024), 0)
    pick = jnp.where(
        jnp.logical_and(lane // 128 == chan // 32, lane % 32 == chan % 32), 1.0, 0.0
    ).astype(BF16)
    quarter = (iota((FEAT, 1024), 1) // 32) % 4

    def spread(w):
        return jnp.concatenate([jnp.where(quarter == q, w, 0.0) for q in range(4)], axis=0).astype(BF16)

    loads[3].wait()
    wc_blk[...] = spread(matmul(wc_ref[...], pick))

    wait_recv(rmid, SWAP)
    piece = pl.ds(slot(T) * SEQ, SEQ)
    local(rmid, r_all.at[:, piece, :], RIGHT)

    @pl.loop(1, N // 2)
    def _(d):
        remote(rmid, r_all.at[:, piece, :], RIGHT, S, (T + 2 * d) % N).start()

    for d in (3, 5, 4):
        send_norm(d)

    loads[4].wait()
    gate = jax.nn.sigmoid(matmul(x_v, spread(matmul(ws_ref[...], pick))))
    gate_scr[...] = gate
    loads[5].wait()
    wf_blk[...] = spread(matmul(wf_ref[...], pick))
    loads[6].wait()
    x_g = by_group(adj_ref[...].astype(F32)).astype(BF16)
    gbuf[...] = (matmul(x_g, wf_blk[...]) * gate).astype(BF16)

    loads[7].wait()
    loads[8].wait()
    m_high, m_low = split(m_scr[...])
    m_hl[:, :128] = m_high
    m_hl[:, 128:] = m_low
    score = score_ref[...]
    repeat = jnp.where(iota((HEADS, 128), 1) // TOK == iota((HEADS, 128), 0), 1.0, 0.0).astype(BF16)

    def repeated(a):
        high, low = split(a)
        return matmul_tn(high, repeat).astype(BF16), matmul_tn(low, repeat).astype(BF16)

    score_high, score_low = repeated(score)
    lane = iota((1, 128), 1) % TOK
    valid = jnp.zeros((1, 128), F32)
    for j in range(TOK):
        valid = jnp.where(lane == j, mask_s[S * TOK + j].astype(F32), valid)
    wait_recv(pin_tile, PAIR_IN)
    pin_scr[...] = pin_tile[...].reshape(TOK * TOK, 128).astype(F32)
    pin = jnp.concatenate([pin_scr[pl.ds(j, TOK, stride=TOK), :] for j in range(TOK)], axis=0)

    half = pl.ds(core * (N // 2) * SEQ, (N // 2) * SEQ)
    wait_recv(r_all.at[:, half, :], RIGHT)
    remote(r_all.at[:, half, :], r_all.at[:, half, :], RIGHT_SIB, S, sibling).start()

    wait_recv(l_all, LEFT)
    wait_recv(r_all.at[:, pl.ds((1 - core) * (N // 2) * SEQ, (N // 2) * SEQ), :], RIGHT_SIB)
    left = jnp.concatenate([l_all[g] for g in range(4)], axis=1)
    right = jnp.concatenate([r_all[g] for g in range(4)], axis=1)
    outer = matmul_tn(left, right)
    for g in range(4):
        o_scr[g] = outer[:, g * 128 : (g + 1) * 128]

    @pl.loop(0, 8)
    def _(cg):
        parts = [
            jnp.concatenate([o_scr[g, pl.ds(4 * cg + q, TOK, stride=32), :] for g in range(4)], axis=0)
            for q in range(4)
        ]
        parts = swap_blocks(parts, 32)
        lanes = pl.ds(pl.multiple_of(cg * 128, 128), 128)
        for j in range(TOK):
            p_scr[pl.ds(j * TOK, TOK), lanes] = parts[j % 4][(j // 4) * TOK : (j // 4 + 1) * TOK]

    p_high, p_low = split(p_scr[...])
    product = matmul(p_high, m_hl[...])
    update = product[:, :128] + (product[:, 128:] + matmul(p_low, m_hl[:, :128]))
    pair_tile = (pin + update).astype(BF16).astype(F32)
    normal = normalize(pair_tile)[0]
    n_high, n_low = split(normal)
    logits = matmul(n_high, score_high) + (matmul(n_high, score_low) + matmul(n_low, score_high))
    own = iota((TOK, 1, 128), 2) % TOK == iota((TOK, 1, 128), 0)
    logits = jnp.sum(jnp.where(own, logits.reshape(TOK, TOK, 128), 0.0), axis=0)
    lg_src[...] = jnp.where(valid > 0, logits, LOW)

    def send_plane(src, dst, phase):
        local(src, dst, phase)

        @pl.loop(1, N)
        def _(d):
            remote(src, dst, phase, (S + d) % N, T).start()

    send_plane(lg_src, lg_all.at[slot(S)], LOGITS)

    po_scr[...] = pair_tile
    for i in range(TOK):
        po_tile[i] = po_scr[pl.ds(i, TOK, stride=TOK), :].astype(BF16)

    @pl.when(y == col)
    def _():
        local(po_tile, po_mid, TURN)

    @pl.when(y != col)
    def _():
        remote(po_tile, po_mid, TURN, col * NC + xpos, row * NC + y).start()

    half = pl.ds(core * (N // 2) * TOK, (N // 2) * TOK)
    wait_recv(nv.at[:, half, :], NORM)
    remote(nv.at[:, half, :], nv.at[:, half, :], NORM_SIB, S, sibling).start()

    wait_recv(po_mid, TURN)
    send_plane(po_mid, po_all.at[pl.ds(y * TOK, TOK), pl.ds(xpos * TOK, TOK), :], PAIR_OUT)

    wait_recv(nv.at[:, pl.ds((1 - core) * (N // 2) * TOK, (N // 2) * TOK), :], NORM_SIB)

    @pl.loop(0, 8)
    def _(g):
        vh[g] = matmul(nv[g], wc_blk[...]).astype(BF16)

    def head(ref, h):
        return [ref[g, :, h * 128 : (h + 1) * 128] for g in range(8)]

    for h in range(HEADS):
        gw = matmul_nt(
            jnp.concatenate([gbuf[g * TOK : (g + 1) * TOK, h * 128 : (h + 1) * 128] for g in range(8)], axis=1),
            jnp.concatenate(head(vh, h), axis=1),
        ).astype(BF16)
        rsbuf[2 * h] = gw[:, :128]
        rsbuf[2 * h + 1] = gw[:, 128:]
    local(rsbuf.at[S], rsrx.at[S], GW_SUM)

    @pl.loop(1, N)
    def _(d):
        s = (S + d) % N
        remote(rsbuf.at[s], rsrx.at[S], GW_SUM, s, T).start()

    wait_recv(lg_all, LOGITS)
    lg = lg_all[...].reshape(2, 8, TOK, 128)
    parts = swap_blocks([lg[:, s].reshape(2 * TOK, 128) for s in range(8)], TOK)
    lg = jnp.stack([jnp.concatenate([a[:TOK], a[TOK:]], axis=1) for a in parts], axis=0)
    scaled = jnp.exp(lg - jnp.max(lg, axis=-1, keepdims=True))
    prob = scaled / jnp.sum(scaled, axis=-1, keepdims=True)
    prob_scr[...] = prob

    wait_recv(rsrx, GW_SUM)
    agbuf[...] = jnp.sum(rsrx[...].astype(F32), axis=0).astype(BF16)
    send_plane(agbuf, agrx.at[S], GW_ALL)

    weights = prob_scr[...].astype(BF16)
    columns = []
    for h in range(HEADS):
        avg = matmul(weights[h], jnp.concatenate(head(vh, h), axis=1))
        avg = jnp.concatenate([avg[:, g * 128 : (g + 1) * 128] for g in range(8)], axis=0)
        columns.append((avg * gate_scr[:, h * 128 : (h + 1) * 128]).astype(BF16))
    mixed = matmul_nt(jnp.concatenate(columns, axis=1), wf_blk[...])
    result = (by_group(x_ref[...].astype(F32)) + mixed).astype(BF16)
    for q in range(4):
        out_al[:, q] = result[:, q * FEAT : (q + 1) * FEAT].reshape(8, TOK, FEAT)

    wait_recv(agrx, GW_ALL)
    gw = agrx[...].astype(F32).reshape(HEADS, 2, TOK, 128)
    gw = jnp.concatenate([gw[:, 0], gw[:, 1]], axis=-1)
    prob = prob_scr[...]
    gl = prob * (gw - jnp.sum(prob * gw, axis=-1, keepdims=True))
    parts = [jnp.concatenate([gl[h, :, :128], gl[h, :, 128:]], axis=0) for h in range(HEADS)]
    parts = swap_blocks(parts, TOK)
    for s in range(N):
        start = (s % 2) * TOK
        glbuf[s // NC, s % NC] = parts[s // 2][start : start + TOK].astype(BF16)
    local(glbuf.at[col], glrx.at[col], GL)

    @pl.loop(1, NC)
    def _(d):
        c = (col + d) % NC
        remote(glbuf.at[c], glrx.at[col], GL, S, row * NC + c).start()

    wait_recv(po_all, PAIR_OUT)
    po_copy = pltpu.make_async_copy(po_all, out_pair, local_sem.at[9])
    po_copy.start()
    center = score - jnp.mean(score, axis=1, keepdims=True)
    c_high, c_low = repeated(center)
    c_hl = jnp.concatenate([c_high, c_low], axis=0)
    own = (iota((1, 1, TOK, 128), 3) % TOK) == iota((1, 1, TOK, 128), 2)
    wait_recv(glrx, GL)
    for c in range(NC):
        for s in range(NC):
            gl_scr[pl.ds(c * TOK, TOK), s] = glrx[c, s].astype(F32).reshape(TOK, 1, 128)
    rows_at_once = 8

    @pl.loop(0, 64 // rows_at_once)
    def _(b):
        rows = pl.ds(b * rows_at_once, rows_at_once)
        block = po_all[rows].reshape(rows_at_once * 64, 128).astype(F32)
        normal, inverse = normalize(block)
        spread_gl = jnp.where(own, gl_scr[rows], 0.0)
        spread_gl = spread_gl.astype(BF16).reshape(rows_at_once * 64, 128)
        grad = matmul_nt(spread_gl, c_hl)
        grad = grad[:, :128] + grad[:, 128:]
        along = jnp.mean(grad * normal, axis=-1, keepdims=True)
        out_grad[rows] = (inverse * (grad - normal * along)).astype(BF16).reshape(rows_at_once, 64, 128)

    po_copy.wait()

    @pl.when(y == col)
    def _():
        wait_send(pair_hbm.at[pl.ds(0, 3 * TOK), pl.ds(0, TOK), :], PAIR_IN)

    @pl.when(y != col)
    def _():
        wait_send(po_tile, TURN)

    @pl.when(S != T)
    def _():
        wait_send(rbuf, SWAP)

    wait_send(l_all.at[:, pl.ds(0, 15 * SEQ), :], LEFT)
    wait_send(r_all.at[:, pl.ds(0, 7 * SEQ), :], RIGHT)
    wait_send(r_all.at[:, pl.ds(0, 8 * SEQ), :], RIGHT_SIB)
    wait_send(nv.at[:, pl.ds(0, 7 * TOK), :], NORM)
    wait_send(nv.at[:, pl.ds(0, 8 * TOK), :], NORM_SIB)
    wait_send(lg_all.at[pl.ds(0, 15)], LOGITS)
    wait_send(po_all.at[pl.ds(0, 60)], PAIR_OUT)
    wait_send(rsrx.at[pl.ds(0, 15)], GW_SUM)
    wait_send(agrx.at[pl.ds(0, 15)], GW_ALL)
    wait_send(glrx.at[pl.ds(0, 3)], GL)


def on_device(
    alignment_input,
    pair_input,
    token_valid_mask,
    first_factor_weights,
    second_factor_weights,
    content_weights_grid,
    sigmoid_weights_grid,
    outer_matrix,
    score_matrix,
    final_mixing_weights,
    adjoint_of_rowset,
):
    vmem = pl.BlockSpec(memory_space=pltpu.VMEM)
    smem = pl.BlockSpec(memory_space=pltpu.SMEM)
    hbm = pl.BlockSpec(memory_space=pltpu.HBM)
    V = pltpu.VMEM
    scratch = [
        V((8, 4, TOK, FEAT), BF16),
        V((8, 4, TOK, FEAT), BF16),
        V((32, FEAT), BF16),
        V((32, FEAT), BF16),
        V((FEAT, 256), BF16),
        V((FEAT, 256), BF16),
        V((FEAT, 256), BF16),
        V((HEADS, 128), F32),
        V((1024, 128), F32),
        V((SEQ * TOK, FEAT), F32),
        V((4, SEQ, 128), BF16),
        V((4, SEQ, 128), BF16),
        V((4, SEQ, 128), BF16),
        V((4, N * SEQ, 128), BF16),
        V((4, N * SEQ, 128), BF16),
        V((8, TOK, 256), BF16),
        V((8, 256, 256), BF16),
        V((8, 256, 1024), BF16),
        V((128, 1024), BF16),
        V((128, 1024), F32),
        V((256, 1024), BF16),
        V((256, 1024), BF16),
        V((1024, 256), BF16),
        V((TOK, TOK, 128), BF16),
        V((TOK * TOK, 128), F32),
        V((4, 512, 128), F32),
        V((256, 1024), F32),
        V((256, 128), F32),
        V((TOK, TOK, 128), BF16),
        V((TOK, TOK, 128), BF16),
        V((64, 64, 128), BF16),
        V((TOK, 128), F32),
        V((N, TOK, 128), F32),
        V((HEADS, TOK, 256), F32),
        V((N, TOK, 128), BF16),
        V((N, TOK, 128), BF16),
        V((TOK, 128), BF16),
        V((N, TOK, 128), BF16),
        V((NC, NC, TOK, 128), BF16),
        V((NC, NC, TOK, 128), BF16),
        V((64, NC, 1, 128), F32),
        pltpu.SemaphoreType.DMA((PHASES,)),
        pltpu.SemaphoreType.DMA((PHASES,)),
        pltpu.SemaphoreType.DMA((10,)),
    ]
    grouped = (8, 4, TOK, FEAT)
    aligned, pair_output, pair_gradient = pl.pallas_call(
        kernel,
        out_shape=[
            jax.ShapeDtypeStruct(grouped, BF16),
            jax.ShapeDtypeStruct((64, 64, 128), BF16),
            jax.ShapeDtypeStruct((64, 64, 128), BF16),
        ],
        in_specs=[smem] + [hbm] * 10,
        out_specs=[vmem, hbm, vmem],
        scratch_shapes=scratch,
        compiler_params=pltpu.CompilerParams(
            collective_id=0, has_side_effects=True, vmem_limit_bytes=60 * 1024 * 1024
        ),
        name="msa_block",
    )(
        token_valid_mask,
        alignment_input.reshape(grouped),
        adjoint_of_rowset.reshape(grouped),
        first_factor_weights.T,
        second_factor_weights.T,
        content_weights_grid,
        sigmoid_weights_grid,
        final_mixing_weights.T,
        score_matrix.T,
        outer_matrix,
        pair_input,
    )
    return aligned.reshape(SEQ, TOK, FEAT), pair_output, pair_gradient


def solution(mesh):
    in_specs = (
        P("seq", ("row", "col"), None),
        P("row", "col", None),
        P(),
        P(),
        P(),
        P(),
        P(),
        P(),
        P(),
        P(),
        P("seq", ("row", "col"), None),
    )
    out_specs = (P("seq", ("row", "col"), None), P("row", "col", None), P("row", "col", None))
    return jax.shard_map(
        on_device, mesh=mesh, in_specs=in_specs, out_specs=out_specs, check_vma=False
    )
```

time: 97.2 us -> 75.1 us (0.77)
  Pallas kernels: 87 us -> 69.4 us
  local copies, waits for them, and re-layouts: 9.08 us -> 4.89 us
    pallas_call x1, Pallas kernels: 87 us -> 69.4 us  [on_device(): pl.pallas_call(kernel, out_shape=[jax.ShapeDtypeStruct(grouped, BF16), ja...]
    unnamed x21 -> x5, local copies, waits for them, and re-layouts: 9.08 us -> 4.89 us
where the time goes in v2:
time: 75.1 us; the launch traced here: 74.9 us
  Pallas kernels  69.4 us (92%)
  local copies, waits for them, and re-layouts  4.89 us (7%)
    pallas_call x1, Pallas kernels, on_device(): pl.pallas_call(kernel, out_shape=[jax.ShapeDtypeStruct(grouped, BF16), ja...  69.4 us
    unnamed x5, local copies, waits for them, and re-layouts  4.89 us

profile of v2, /device:TPU:1, one launch (start us, length us, event | category | flops | bytes accessed | tf_op | source)
XLA Modules:
  0.0 74.9 jit_solution(8825916211438617375)
XLA Ops:
  0.6 69.4 %msa_block.1 = (bf16[8,4,16,64]{3,2,1,0:T(8,128)(2,1)}, bf16[64,64,128]{2,1,0:T(8,128)(2,1)}, bf16[64,64,128]{2,1,0:T(8,128)(2,1)}) custom-call(s32[256]{0:T(256)} %mask_s.1, bf16[8,4,16,64]{3,2,1,0:T(8,128)(2,1)} %bitcast.7, bf16[8,4,16,64]{3,2,1,0:T(8,128)(2,1)} %bitcast.8, bf16[32,64]{1,0:T(8,128)(2,1)} %bitcast.11, bf16[32,64]{1,0:T(8,128)(2,1)} %bitcast.12, ...), custom_call_target="tpu_custom_call" | custom-call | tf_op jit(solution)/shard_map/msa_block/pallas_call | solution.py:517
  70.0 1.6 %copy.17 = bf16[32,16,64]{2,1,0:T(8,128)(2,1)} copy(bf16[32,16,64]{2,1,0:T(8,128)(2,1)} %bitcast.9) | data formatting | bytes 131072
  71.6 0.0 copy-start
  71.6 2.4 %copy.18 = bf16[64,64,128]{2,1,0:T(8,128)(2,1)} copy(bf16[64,64,128]{2,1,0:T(8,128)(2,1)} %get-tuple-element.13) | data formatting | bytes 2097152
  73.9 0.0 copy-done
  73.9 1.0 %copy.19 = bf16[64,64,128]{2,1,0:T(8,128)(2,1)} copy(bf16[64,64,128]{2,1,0:T(8,128)(2,1)S(1)} %copy-done) | data formatting | bytes 2097152
Async XLA Ops:
  71.6 2.4 %copy-start = (bf16[64,64,128]{2,1,0:T(8,128)(2,1)S(1)}, bf16[64,64,128]{2,1,0:T(8,128)(2,1)}, u32[]{:S(2)}) copy-start(bf16[64,64,128]{2,1,0:T(8,128)(2,1)} %get-tuple-element.14) | copy-start | bytes 3145732

commit v3 on v2

--- a/solution.py
+++ b/solution.py
@@ -19,8 +19,8 @@
 HEADS = 8
 FEAT = 64
 
-PAIR_IN, LEFT, SWAP, RIGHT, RIGHT_SIB, NORM, NORM_SIB, LOGITS, TURN, PAIR_OUT, GW_SUM, GW_ALL, GL = range(13)
-PHASES = 13
+PAIR_IN, LEFT, RIGHT, RIGHT_SIB, NORM, NORM_SIB, LOGITS, TURN, A1, B1, A2, B2, GL_SUM, GL = range(14)
+PHASES = 14
 
 
 def iota(shape, dim):
@@ -69,11 +69,11 @@
 
 def kernel(
     mask_s, x_hbm, adj_hbm, w1_hbm, w2_hbm, wc_hbm, ws_hbm, wf_hbm, score_hbm, m_hbm, pair_hbm,
-    out_al, out_pair, out_grad,
+    out_al, out_pair, out_gl,
     x_ref, adj_ref, w1_ref, w2_ref, wc_ref, ws_ref, wf_ref, score_ref, m_scr,
-    xn_scr, lbuf, rbuf, rmid, l_all, r_all, nbuf, nv, vh, gbuf, gate_scr, wc_blk, wf_blk, m_hl,
+    xn_scr, lbuf, rbuf, l_all, r_all, nbuf, nv, vh, gbuf, gate_scr, wc_blk, wf_blk, m_hl,
     pin_tile, pin_scr, o_scr, p_scr, po_scr, po_tile, po_mid, po_all, lg_src, lg_all, prob_scr,
-    rsbuf, rsrx, agbuf, agrx, glbuf, glrx, gl_scr,
+    rsbuf, rsrx, gl_tile, gl_all,
     send_sem, recv_sem, local_sem,
 ):
     S = lax.axis_index("seq")
@@ -122,30 +122,26 @@
     def greet(s, t):
         pl.semaphore_signal(barrier, inc=1, device_id=device(s, t), device_id_type=MESH)
 
-    @pl.loop(1, N)
-    def _(d):
+    for d in range(1, N):
         greet((S + d) % N, T)
-
-    @pl.loop(1, N // 2)
-    def _(d):
+    for d in range(1, N // 2):
         greet(S, (T + 2 * d) % N)
-
     greet(S, sibling)
-
-    @pl.loop(1, NC)
-    def _(d):
-        greet(S, row * NC + (col + d) % NC)
-
-    @pl.when(S != T)
-    def _():
-        greet(T, S)
-
-    @pl.when(y != col)
-    def _():
-        greet(col * NC + xpos, row * NC + y)
-
-    greeted = N - 1 + N // 2 - 1 + 1 + NC - 1
-    greeted = greeted + jnp.where(S != T, 1, 0).astype(I32) + jnp.where(y != col, 1, 0).astype(I32)
+    across = (sibling + 2) % 4
+    greet(S, row * NC + across)
+
+    def right_source(d):
+        return (core + 2 * d + 2 * (S // 2)) % N
+
+    for d in range(1, N // 2):
+        greet(right_source(d), S)
+
+    @pl.when(jnp.logical_or(right_source(0) != S, S != T))
+    def _():
+        greet(right_source(0), S)
+
+    alone = jnp.logical_and(S == T, S % 2 == core)
+    greeted = N - 1 + N // 2 - 1 + 2 + N // 2 - jnp.where(alone, 1, 0).astype(I32)
 
     loads[0].wait()
     xn = normalize(x_ref[...].reshape(SEQ * TOK, FEAT).astype(F32))[0].astype(BF16).astype(F32)
@@ -183,29 +179,27 @@
 
     pl.semaphore_wait(barrier, greeted)
 
-    @pl.when(S == T)
-    def _():
-        local(rbuf, rmid, SWAP)
-
-    @pl.when(S != T)
-    def _():
-        remote(rbuf, rmid, SWAP, T, S).start()
-
-    mine = pl.ds(slot(S) * SEQ, SEQ)
-    local(lbuf, l_all.at[:, mine, :], LEFT)
+    parity = S % 2
+
+    def send_right(d):
+        remote(rbuf, r_all.at[slot(S)], RIGHT, T, (T - core + parity + 2 * d) % N).start()
+
+    for d in (4, 3, 5, 2, 6, 1, 7):
+        send_right(d)
+
+    @pl.when(alone)
+    def _():
+        local(rbuf, r_all.at[slot(S)], RIGHT)
+
+    @pl.when(jnp.logical_not(alone))
+    def _():
+        send_right(0)
+
+    local(lbuf, l_all.at[slot(S)], LEFT)
 
     @pl.loop(1, N)
     def _(d):
-        remote(lbuf, l_all.at[:, mine, :], LEFT, (S + d) % N, T).start()
-
-    tokens = pl.ds(slot(T) * TOK, TOK)
-
-    def send_norm(d):
-        remote(nbuf, nv.at[:, tokens, :], NORM, S, (T + 2 * d) % N).start()
-
-    local(nbuf, nv.at[:, tokens, :], NORM)
-    for d in (1, 7, 2, 6):
-        send_norm(d)
+        remote(lbuf, l_all.at[slot(S)], LEFT, (S + d) % N, T).start()
 
     my_tile = pair_hbm.at[pl.ds(col * TOK, TOK), pl.ds(xpos * TOK, TOK), :]
 
@@ -220,6 +214,10 @@
                 pair_hbm.at[pl.ds(c * TOK, TOK), pl.ds(xpos * TOK, TOK), :], pin_tile, PAIR_IN, S, row * NC + c
             ).start()
 
+    local(nbuf, nv.at[slot(T)], NORM)
+    for d in (4, 3, 5, 2, 6, 1, 7):
+        remote(nbuf, nv.at[slot(T)], NORM, S, (T + 2 * d) % N).start()
+
     lane = iota((256, 1024), 1)
     chan = iota((256, 1024), 0)
     pick = jnp.where(
@@ -232,17 +230,6 @@
 
     loads[3].wait()
     wc_blk[...] = spread(matmul(wc_ref[...], pick))
-
-    wait_recv(rmid, SWAP)
-    piece = pl.ds(slot(T) * SEQ, SEQ)
-    local(rmid, r_all.at[:, piece, :], RIGHT)
-
-    @pl.loop(1, N // 2)
-    def _(d):
-        remote(rmid, r_all.at[:, piece, :], RIGHT, S, (T + 2 * d) % N).start()
-
-    for d in (3, 5, 4):
-        send_norm(d)
 
     loads[4].wait()
     gate = jax.nn.sigmoid(matmul(x_v, spread(matmul(ws_ref[...], pick))))
@@ -274,14 +261,15 @@
     pin_scr[...] = pin_tile[...].reshape(TOK * TOK, 128).astype(F32)
     pin = jnp.concatenate([pin_scr[pl.ds(j, TOK, stride=TOK), :] for j in range(TOK)], axis=0)
 
-    half = pl.ds(core * (N // 2) * SEQ, (N // 2) * SEQ)
-    wait_recv(r_all.at[:, half, :], RIGHT)
-    remote(r_all.at[:, half, :], r_all.at[:, half, :], RIGHT_SIB, S, sibling).start()
+    half = pl.ds(core * (N // 2), N // 2)
+    other = pl.ds((1 - core) * (N // 2), N // 2)
+    wait_recv(r_all.at[half], RIGHT)
+    remote(r_all.at[half], r_all.at[half], RIGHT_SIB, S, sibling).start()
 
     wait_recv(l_all, LEFT)
-    wait_recv(r_all.at[:, pl.ds((1 - core) * (N // 2) * SEQ, (N // 2) * SEQ), :], RIGHT_SIB)
-    left = jnp.concatenate([l_all[g] for g in range(4)], axis=1)
-    right = jnp.concatenate([r_all[g] for g in range(4)], axis=1)
+    left = jnp.concatenate([l_all[:, g].reshape(N * SEQ, 128) for g in range(4)], axis=1)
+    wait_recv(r_all.at[other], RIGHT_SIB)
+    right = jnp.concatenate([r_all[:, g].reshape(N * SEQ, 128) for g in range(4)], axis=1)
     outer = matmul_tn(left, right)
     for g in range(4):
         o_scr[g] = outer[:, g * 128 : (g + 1) * 128]
@@ -329,35 +317,27 @@
     def _():
         remote(po_tile, po_mid, TURN, col * NC + xpos, row * NC + y).start()
 
-    half = pl.ds(core * (N // 2) * TOK, (N // 2) * TOK)
-    wait_recv(nv.at[:, half, :], NORM)
-    remote(nv.at[:, half, :], nv.at[:, half, :], NORM_SIB, S, sibling).start()
+    wait_recv(nv.at[half], NORM)
+    remote(nv.at[half], nv.at[half], NORM_SIB, S, sibling).start()
+
+    def values(start):
+        @pl.loop(0, 4)
+        def _(n):
+            blocks = pl.ds(start + 2 * n, 2)
+            rows = nv[blocks].reshape(2 * 8 * TOK, 256)
+            vh[blocks] = matmul(rows, wc_blk[...]).astype(BF16).reshape(2, 8, TOK, 1024)
+
+    values(core * (N // 2))
 
     wait_recv(po_mid, TURN)
-    send_plane(po_mid, po_all.at[pl.ds(y * TOK, TOK), pl.ds(xpos * TOK, TOK), :], PAIR_OUT)
-
-    wait_recv(nv.at[:, pl.ds((1 - core) * (N // 2) * TOK, (N // 2) * TOK), :], NORM_SIB)
-
-    @pl.loop(0, 8)
-    def _(g):
-        vh[g] = matmul(nv[g], wc_blk[...]).astype(BF16)
-
-    def head(ref, h):
-        return [ref[g, :, h * 128 : (h + 1) * 128] for g in range(8)]
-
-    for h in range(HEADS):
-        gw = matmul_nt(
-            jnp.concatenate([gbuf[g * TOK : (g + 1) * TOK, h * 128 : (h + 1) * 128] for g in range(8)], axis=1),
-            jnp.concatenate(head(vh, h), axis=1),
-        ).astype(BF16)
-        rsbuf[2 * h] = gw[:, :128]
-        rsbuf[2 * h + 1] = gw[:, 128:]
-    local(rsbuf.at[S], rsrx.at[S], GW_SUM)
-
-    @pl.loop(1, N)
-    def _(d):
-        s = (S + d) % N
-        remote(rsbuf.at[s], rsrx.at[S], GW_SUM, s, T).start()
+    top, low = pl.ds(0, TOK // 2), pl.ds(TOK // 2, TOK // 2)
+    across_x = pl.ds(xpos * TOK, TOK)
+    own_a, own_b = po_all.at[y, top, across_x, :], po_all.at[y, low, across_x, :]
+    local(po_mid.at[top], own_a, A1)
+    local(po_mid.at[low], own_b, B1)
+    for d in (1, 3, 2):
+        remote(po_mid.at[top], own_a, A1, y * NC + (xpos + d) % NC, T).start()
+        remote(po_mid.at[low], own_b, B1, (S + NC * d) % N, T).start()
 
     wait_recv(lg_all, LOGITS)
     lg = lg_all[...].reshape(2, 8, TOK, 128)
@@ -367,9 +347,39 @@
     prob = scaled / jnp.sum(scaled, axis=-1, keepdims=True)
     prob_scr[...] = prob
 
-    wait_recv(rsrx, GW_SUM)
-    agbuf[...] = jnp.sum(rsrx[...].astype(F32), axis=0).astype(BF16)
-    send_plane(agbuf, agrx.at[S], GW_ALL)
+    wait_recv(nv.at[other], NORM_SIB)
+    values((1 - core) * (N // 2))
+
+    def head(ref, h):
+        return [ref[:, g, :, h * 128 : (h + 1) * 128].reshape(256, 128) for g in range(8)]
+
+    gl = []
+    for h in range(HEADS):
+        gw = matmul_nt(
+            jnp.concatenate([gbuf[g * TOK : (g + 1) * TOK, h * 128 : (h + 1) * 128] for g in range(8)], axis=1),
+            jnp.concatenate(head(vh, h), axis=1),
+        )
+        prob = prob_scr[h]
+        gl.append(prob * (gw - jnp.sum(prob * gw, axis=-1, keepdims=True)))
+    parts = swap_blocks([jnp.concatenate([a[:, :128], a[:, 128:]], axis=0) for a in gl], TOK)
+    for s in range(N):
+        start = (s % 2) * TOK
+        rsbuf[s] = parts[s // 2][start : start + TOK].astype(BF16)
+    local(rsbuf.at[S], rsrx.at[S], GL_SUM)
+
+    @pl.loop(1, N)
+    def _(d):
+        s = (S + d) % N
+        remote(rsbuf.at[s], rsrx.at[S], GL_SUM, s, T).start()
+
+    lines = po_all.at[y, top]
+    wait_recv(lines, A1)
+    for d in (1, 3, 2):
+        remote(lines, lines, A2, (S + NC * d) % N, T).start()
+    stripe = po_all.at[:, low, across_x, :]
+    wait_recv(stripe, B1)
+    for d in (1, 3, 2):
+        remote(stripe, stripe, B2, y * NC + (xpos + d) % NC, T).start()
 
     weights = prob_scr[...].astype(BF16)
     columns = []
@@ -382,72 +392,84 @@
     for q in range(4):
         out_al[:, q] = result[:, q * FEAT : (q + 1) * FEAT].reshape(8, TOK, FEAT)
 
-    wait_recv(agrx, GW_ALL)
-    gw = agrx[...].astype(F32).reshape(HEADS, 2, TOK, 128)
-    gw = jnp.concatenate([gw[:, 0], gw[:, 1]], axis=-1)
-    prob = prob_scr[...]
-    gl = prob * (gw - jnp.sum(prob * gw, axis=-1, keepdims=True))
-    parts = [jnp.concatenate([gl[h, :, :128], gl[h, :, 128:]], axis=0) for h in range(HEADS)]
-    parts = swap_blocks(parts, TOK)
-    for s in range(N):
-        start = (s % 2) * TOK
-        glbuf[s // NC, s % NC] = parts[s // 2][start : start + TOK].astype(BF16)
-    local(glbuf.at[col], glrx.at[col], GL)
-
-    @pl.loop(1, NC)
+    wait_recv(rsrx, GL_SUM)
+    gl_tile[...] = jnp.sum(rsrx[...].astype(F32), axis=0).astype(BF16)
+    place = gl_all.at[col, xpos]
+    owner = row * NC + y
+
+    @pl.when(y == col)
+    def _():
+        local(gl_tile, place, GL)
+
+    @pl.when(y != col)
+    def _():
+        remote(gl_tile, place, GL, S, owner).start()
+
+    @pl.loop(1, N)
     def _(d):
-        c = (col + d) % NC
-        remote(glbuf.at[c], glrx.at[col], GL, S, row * NC + c).start()
-
-    wait_recv(po_all, PAIR_OUT)
+        remote(gl_tile, place, GL, (S + d) % N, owner).start()
+
+    wait_recv(po_all.at[pl.ds(0, 3), top], A2)
+    wait_recv(po_all.at[pl.ds(0, 3), low], B2)
     po_copy = pltpu.make_async_copy(po_all, out_pair, local_sem.at[9])
     po_copy.start()
-    center = score - jnp.mean(score, axis=1, keepdims=True)
-    c_high, c_low = repeated(center)
-    c_hl = jnp.concatenate([c_high, c_low], axis=0)
+    wait_recv(gl_all, GL)
+    out_gl[...] = gl_all[...]
+    po_copy.wait()
+
+    @pl.when(y == col)
+    def _():
+        wait_send(pair_hbm.at[pl.ds(0, 3 * TOK), pl.ds(0, TOK), :], PAIR_IN)
+        wait_send(rsrx.at[pl.ds(0, 15)], GL)
+
+    @pl.when(y != col)
+    def _():
+        wait_send(po_tile, TURN)
+        wait_send(rsrx, GL)
+
+    @pl.when(alone)
+    def _():
+        wait_send(r_all.at[pl.ds(0, 7)], RIGHT)
+
+    @pl.when(jnp.logical_not(alone))
+    def _():
+        wait_send(r_all.at[pl.ds(0, 8)], RIGHT)
+
+    wait_send(l_all.at[pl.ds(0, 15)], LEFT)
+    wait_send(r_all.at[pl.ds(0, 8)], RIGHT_SIB)
+    wait_send(nv.at[pl.ds(0, 7)], NORM)
+    wait_send(nv.at[pl.ds(0, 8)], NORM_SIB)
+    wait_send(lg_all.at[pl.ds(0, 15)], LOGITS)
+    wait_send(po_all.at[0, pl.ds(0, 8), pl.ds(0, 48), :], A1)
+    wait_send(po_all.at[0, pl.ds(0, 8), pl.ds(0, 48), :], B1)
+    wait_send(po_all.at[pl.ds(0, 3), top], A2)
+    wait_send(po_all.at[pl.ds(0, 3), low], B2)
+    wait_send(rsrx.at[pl.ds(0, 15)], GL_SUM)
+
+
+def finish_kernel(po_ref, gl_ref, score_ref, al_ref, out_al, out_pair, out_grad, gl_scr, c_hl):
+    @pl.when(pl.program_id(0) == 0)
+    def _():
+        score = score_ref[...]
+        repeat = jnp.where(iota((HEADS, 128), 1) // TOK == iota((HEADS, 128), 0), 1.0, 0.0).astype(BF16)
+        high, low = split(score - jnp.mean(score, axis=1, keepdims=True))
+        c_hl[:128] = matmul_tn(high, repeat).astype(BF16)
+        c_hl[128:] = matmul_tn(low, repeat).astype(BF16)
+
+    out_al[...] = al_ref[...]
+    out_pair[...] = po_ref[...]
+    for s in range(NC):
+        gl_scr[:, s] = gl_ref[0, s].astype(F32).reshape(TOK, 1, 128)
     own = (iota((1, 1, TOK, 128), 3) % TOK) == iota((1, 1, TOK, 128), 2)
-    wait_recv(glrx, GL)
-    for c in range(NC):
-        for s in range(NC):
-            gl_scr[pl.ds(c * TOK, TOK), s] = glrx[c, s].astype(F32).reshape(TOK, 1, 128)
-    rows_at_once = 8
-
-    @pl.loop(0, 64 // rows_at_once)
-    def _(b):
-        rows = pl.ds(b * rows_at_once, rows_at_once)
-        block = po_all[rows].reshape(rows_at_once * 64, 128).astype(F32)
-        normal, inverse = normalize(block)
-        spread_gl = jnp.where(own, gl_scr[rows], 0.0)
-        spread_gl = spread_gl.astype(BF16).reshape(rows_at_once * 64, 128)
-        grad = matmul_nt(spread_gl, c_hl)
+    part = TOK // 2
+    for b in range(2):
+        rows = pl.ds(b * part, part)
+        normal, inverse = normalize(po_ref[rows].reshape(part * 64, 128).astype(F32))
+        lhs = jnp.where(own, gl_scr[rows], 0.0).astype(BF16).reshape(part * 64, 128)
+        grad = matmul_nt(lhs, c_hl[...])
         grad = grad[:, :128] + grad[:, 128:]
         along = jnp.mean(grad * normal, axis=-1, keepdims=True)
-        out_grad[rows] = (inverse * (grad - normal * along)).astype(BF16).reshape(rows_at_once, 64, 128)
-
-    po_copy.wait()
-
-    @pl.when(y == col)
-    def _():
-        wait_send(pair_hbm.at[pl.ds(0, 3 * TOK), pl.ds(0, TOK), :], PAIR_IN)
-
-    @pl.when(y != col)
-    def _():
-        wait_send(po_tile, TURN)
-
-    @pl.when(S != T)
-    def _():
-        wait_send(rbuf, SWAP)
-
-    wait_send(l_all.at[:, pl.ds(0, 15 * SEQ), :], LEFT)
-    wait_send(r_all.at[:, pl.ds(0, 7 * SEQ), :], RIGHT)
-    wait_send(r_all.at[:, pl.ds(0, 8 * SEQ), :], RIGHT_SIB)
-    wait_send(nv.at[:, pl.ds(0, 7 * TOK), :], NORM)
-    wait_send(nv.at[:, pl.ds(0, 8 * TOK), :], NORM_SIB)
-    wait_send(lg_all.at[pl.ds(0, 15)], LOGITS)
-    wait_send(po_all.at[pl.ds(0, 60)], PAIR_OUT)
-    wait_send(rsrx.at[pl.ds(0, 15)], GW_SUM)
-    wait_send(agrx.at[pl.ds(0, 15)], GW_ALL)
-    wait_send(glrx.at[pl.ds(0, 3)], GL)
+        out_grad[rows] = (inverse * (grad - normal * along)).astype(BF16).reshape(part, 64, 128)
 
 
 def on_device(
@@ -480,12 +502,11 @@
         V((SEQ * TOK, FEAT), F32),
         V((4, SEQ, 128), BF16),
         V((4, SEQ, 128), BF16),
-        V((4, SEQ, 128), BF16),
-        V((4, N * SEQ, 128), BF16),
-        V((4, N * SEQ, 128), BF16),
+        V((N, 4, SEQ, 128), BF16),
+        V((N, 4, SEQ, 128), BF16),
         V((8, TOK, 256), BF16),
-        V((8, 256, 256), BF16),
-        V((8, 256, 1024), BF16),
+        V((N, 8, TOK, 256), BF16),
+        V((N, 8, TOK, 1024), BF16),
         V((128, 1024), BF16),
         V((128, 1024), F32),
         V((256, 1024), BF16),
@@ -498,28 +519,25 @@
         V((256, 128), F32),
         V((TOK, TOK, 128), BF16),
         V((TOK, TOK, 128), BF16),
-        V((64, 64, 128), BF16),
+        V((NC, TOK, 64, 128), BF16),
         V((TOK, 128), F32),
         V((N, TOK, 128), F32),
         V((HEADS, TOK, 256), F32),
         V((N, TOK, 128), BF16),
         V((N, TOK, 128), BF16),
         V((TOK, 128), BF16),
-        V((N, TOK, 128), BF16),
         V((NC, NC, TOK, 128), BF16),
-        V((NC, NC, TOK, 128), BF16),
-        V((64, NC, 1, 128), F32),
         pltpu.SemaphoreType.DMA((PHASES,)),
         pltpu.SemaphoreType.DMA((PHASES,)),
         pltpu.SemaphoreType.DMA((10,)),
     ]
     grouped = (8, 4, TOK, FEAT)
-    aligned, pair_output, pair_gradient = pl.pallas_call(
+    aligned, pair_block, grad_logits = pl.pallas_call(
         kernel,
         out_shape=[
             jax.ShapeDtypeStruct(grouped, BF16),
-            jax.ShapeDtypeStruct((64, 64, 128), BF16),
-            jax.ShapeDtypeStruct((64, 64, 128), BF16),
+            jax.ShapeDtypeStruct((NC, TOK, 64, 128), BF16),
+            jax.ShapeDtypeStruct((NC, NC, TOK, 128), BF16),
         ],
         in_specs=[smem] + [hbm] * 10,
         out_specs=[vmem, hbm, vmem],
@@ -541,6 +559,27 @@
         outer_matrix,
         pair_input,
     )
+    rows = pl.BlockSpec((TOK, 64, 128), lambda n: (n, 0, 0))
+    groups = pl.BlockSpec((2, 4, TOK, FEAT), lambda n: (n, 0, 0, 0))
+    aligned, pair_output, pair_gradient = pl.pallas_call(
+        finish_kernel,
+        grid=(NC,),
+        out_shape=[
+            jax.ShapeDtypeStruct(grouped, BF16),
+            jax.ShapeDtypeStruct((64, 64, 128), BF16),
+            jax.ShapeDtypeStruct((64, 64, 128), BF16),
+        ],
+        in_specs=[
+            rows,
+            pl.BlockSpec((1, NC, TOK, 128), lambda n: (n, 0, 0, 0)),
+            pl.BlockSpec((HEADS, 128), lambda n: (0, 0)),
+            groups,
+        ],
+        out_specs=[groups, rows, rows],
+        scratch_shapes=[V((TOK, NC, 1, 128), F32), V((256, 128), BF16)],
+        compiler_params=pltpu.CompilerParams(vmem_limit_bytes=60 * 1024 * 1024),
+        name="pair_gradient",
+    )(pair_block.reshape(64, 64, 128), grad_logits, score_matrix.T, aligned)
     return aligned.reshape(SEQ, TOK, FEAT), pair_output, pair_gradient
 
 

time: 75.1 us -> 55.2 us (0.74)
  Pallas kernels: 69.4 us -> 54.1 us
  local copies, waits for them, and re-layouts: 4.89 us -> 0 us
    pallas_call x1, Pallas kernels: 69.4 us -> 49.2 us  [on_device(): pl.pallas_call(kernel, out_shape=[jax.ShapeDtypeStruct(grouped, BF16), ja...]
    unnamed x5 -> x0, local copies, waits for them, and re-layouts: 4.89 us -> none
    pallas_call x0 -> x1, Pallas kernels: none -> 4.86 us  [on_device(): pl.pallas_call(finish_kernel, grid=(NC,), out_shape=[jax.ShapeDtypeStruct...]
where the time goes in v3:
time: 55.2 us; the launch traced here: 54.7 us
  Pallas kernels  54.1 us (98%)
  between operations  0.64 us (1%)
    pallas_call x1, Pallas kernels, on_device(): pl.pallas_call(kernel, out_shape=[jax.ShapeDtypeStruct(grouped, BF16), ja...  49.2 us
    pallas_call x1, Pallas kernels, on_device(): pl.pallas_call(finish_kernel, grid=(NC,), out_shape=[jax.ShapeDtypeStruct...  4.86 us

profile of v3, /device:TPU:1, one launch (start us, length us, event | category | flops | bytes accessed | tf_op | source)
XLA Modules:
  0.0 54.7 jit_solution(11819663426949706980)
XLA Ops:
  0.6 49.2 %msa_block.1 = (bf16[8,4,16,64]{3,2,1,0:T(8,128)(2,1)}, bf16[4,16,64,128]{3,2,1,0:T(8,128)(2,1)}, bf16[4,4,16,128]{3,2,1,0:T(8,128)(2,1)}) custom-call(s32[256]{0:T(256)} %mask_s.1, bf16[8,4,16,64]{3,2,1,0:T(8,128)(2,1)} %bitcast.9, bf16[8,4,16,64]{3,2,1,0:T(8,128)(2,1)} %bitcast.10, bf16[32,64]{1,0:T(8,128)(2,1)} %bitcast.14, bf16[32,64]{1,0:T(8,128)(2,1)} %bitcast.15, ...), custom_call_target="tpu_custom_call" | custom-call | tf_op jit(solution)/shard_map/msa_block/pallas_call | solution.py:535
  49.9 4.9 %pair_gradient.1 = (bf16[8,4,16,64]{3,2,1,0:T(8,128)(2,1)}, bf16[64,64,128]{2,1,0:T(8,128)(2,1)}, bf16[64,64,128]{2,1,0:T(8,128)(2,1)}) custom-call(bf16[64,64,128]{2,1,0:T(8,128)(2,1)} %bitcast.8, bf16[4,4,16,128]{3,2,1,0:T(8,128)(2,1)} %get-tuple-element.10.gl_ref, f32[8,128]{1,0:T(8,128)} %bitcast.13, bf16[8,4,16,64]{3,2,1,0:T(8,128)(2,1)} %get-tuple-element.11.al_ref), custom_call_target="tpu_custom_call" | custom-call | tf_op jit(solution)/shard_map/pair_gradient/pallas_call | solution.py:564

commit v4 on v3

--- a/solution.py
+++ b/solution.py
@@ -19,8 +19,9 @@
 HEADS = 8
 FEAT = 64
 
-PAIR_IN, LEFT, RIGHT, RIGHT_SIB, NORM, NORM_SIB, LOGITS, TURN, A1, B1, A2, B2, GL_SUM, GL = range(14)
-PHASES = 14
+PAIR_IN, LEFT, RIGHT, RIGHT_SIB, NORM, NORM_SIB, FAR, FAR_SIB, LOGITS, TURN, A1, B1, A2, B2, GL_SUM, GL = range(16)
+PHASES = 16
+FAR_FIRST = (10, 6, 14, 9, 11, 2, 8, 5, 7, 13, 15, 1, 3, 4, 12)
 
 
 def iota(shape, dim):
@@ -107,15 +108,24 @@
         pltpu.make_async_copy(buf, buf, send_sem.at[phase]).wait()
 
     loads = []
-    for n, (src, dst) in enumerate(
-        [
-            (x_hbm, x_ref), (w1_hbm, w1_ref), (w2_hbm, w2_ref), (wc_hbm, wc_ref), (ws_hbm, ws_ref),
-            (wf_hbm, wf_ref), (adj_hbm, adj_ref), (score_hbm, score_ref), (m_hbm, m_scr),
-        ]
-    ):
-        copy = pltpu.make_async_copy(src, dst, local_sem.at[n])
-        copy.start()
-        loads.append(copy)
+
+    def load(*pairs):
+        for src, dst in pairs:
+            copy = pltpu.make_async_copy(src, dst, local_sem.at[len(loads)])
+            copy.start()
+            loads.append(copy)
+
+    load((x_hbm, x_ref), (w1_hbm, w1_ref), (w2_hbm, w2_ref))
+    load(
+        (wc_hbm, wc_ref), (ws_hbm, ws_ref), (wf_hbm, wf_ref), (adj_hbm, adj_ref), (score_hbm, score_ref), (m_hbm, m_scr)
+    )
+
+
+    plane_x = [(xpos + d) % NC for d in range(NC)]
+    plane_y = [(y + d) % NC * NC for d in range(NC)]
+
+    def plane(d):
+        return plane_y[d // NC] + plane_x[d % NC]
 
     barrier = pltpu.get_barrier_semaphore()
 
@@ -150,9 +160,6 @@
     def by_group(a):
         a = a.reshape(8, 4, TOK, FEAT)
         return jnp.concatenate([a[:, q].reshape(8 * TOK, FEAT) for q in range(4)], axis=1)
-
-    x_v = by_group(xn).astype(BF16)
-    nbuf[...] = x_v.reshape(8, TOK, 256)
 
     loads[1].wait()
     loads[2].wait()
@@ -197,9 +204,8 @@
 
     local(lbuf, l_all.at[slot(S)], LEFT)
 
-    @pl.loop(1, N)
-    def _(d):
-        remote(lbuf, l_all.at[slot(S)], LEFT, (S + d) % N, T).start()
+    for d in FAR_FIRST:
+        remote(lbuf, l_all.at[slot(S)], LEFT, plane(d), T).start()
 
     my_tile = pair_hbm.at[pl.ds(col * TOK, TOK), pl.ds(xpos * TOK, TOK), :]
 
@@ -214,8 +220,10 @@
                 pair_hbm.at[pl.ds(c * TOK, TOK), pl.ds(xpos * TOK, TOK), :], pin_tile, PAIR_IN, S, row * NC + c
             ).start()
 
+    x_v = by_group(xn).astype(BF16)
+    nbuf[...] = x_v.reshape(8, TOK, 256)
     local(nbuf, nv.at[slot(T)], NORM)
-    for d in (4, 3, 5, 2, 6, 1, 7):
+    for d in (2, 6, 1, 7):
         remote(nbuf, nv.at[slot(T)], NORM, S, (T + 2 * d) % N).start()
 
     lane = iota((256, 1024), 1)
@@ -266,15 +274,17 @@
     wait_recv(r_all.at[half], RIGHT)
     remote(r_all.at[half], r_all.at[half], RIGHT_SIB, S, sibling).start()
 
+    def factors_of(ref, part):
+        return jnp.concatenate([ref[part, g].reshape(N // 2 * SEQ, 128) for g in range(4)], axis=1)
+
     wait_recv(l_all, LEFT)
-    left = jnp.concatenate([l_all[:, g].reshape(N * SEQ, 128) for g in range(4)], axis=1)
+    outer = matmul_tn(factors_of(l_all, half), factors_of(r_all, half))
     wait_recv(r_all.at[other], RIGHT_SIB)
-    right = jnp.concatenate([r_all[:, g].reshape(N * SEQ, 128) for g in range(4)], axis=1)
-    outer = matmul_tn(left, right)
+    outer += matmul_tn(factors_of(l_all, other), factors_of(r_all, other))
     for g in range(4):
         o_scr[g] = outer[:, g * 128 : (g + 1) * 128]
 
-    @pl.loop(0, 8)
+    @pl.loop(0, 8, unroll=True)
     def _(cg):
         parts = [
             jnp.concatenate([o_scr[g, pl.ds(4 * cg + q, TOK, stride=32), :] for g in range(4)], axis=0)
@@ -297,11 +307,9 @@
     lg_src[...] = jnp.where(valid > 0, logits, LOW)
 
     def send_plane(src, dst, phase):
+        for d in FAR_FIRST:
+            remote(src, dst, phase, plane(d), T).start()
         local(src, dst, phase)
-
-        @pl.loop(1, N)
-        def _(d):
-            remote(src, dst, phase, (S + d) % N, T).start()
 
     send_plane(lg_src, lg_all.at[slot(S)], LOGITS)
 
@@ -317,17 +325,20 @@
     def _():
         remote(po_tile, po_mid, TURN, col * NC + xpos, row * NC + y).start()
 
-    wait_recv(nv.at[half], NORM)
-    remote(nv.at[half], nv.at[half], NORM_SIB, S, sibling).start()
-
-    def values(start):
-        @pl.loop(0, 4)
-        def _(n):
-            blocks = pl.ds(start + 2 * n, 2)
-            rows = nv[blocks].reshape(2 * 8 * TOK, 256)
-            vh[blocks] = matmul(rows, wc_blk[...]).astype(BF16).reshape(2, 8, TOK, 1024)
-
-    values(core * (N // 2))
+    chip = T // 2
+
+    def place(d, swap=0):
+        c = core + swap - 2 * swap * core
+        return c * (N // 2) + (chip + d) % (N // 2)
+
+    wait_recv(nv.at[pl.ds(0, 5)], NORM)
+    for d, far in ((6, 2), (6, 1), (2, 7)):
+        block = nv.at[place(d)]
+        remote(block, block, FAR, S, (T + 2 * far) % N).start()
+    near = (0, 1, 2, 6, 7)
+    for d in near:
+        block = nv.at[place(d)]
+        remote(block, block, NORM_SIB, S, sibling).start()
 
     wait_recv(po_mid, TURN)
     top, low = pl.ds(0, TOK // 2), pl.ds(TOK // 2, TOK // 2)
@@ -339,6 +350,14 @@
         remote(po_mid.at[top], own_a, A1, y * NC + (xpos + d) % NC, T).start()
         remote(po_mid.at[low], own_b, B1, (S + NC * d) % N, T).start()
 
+    def values(blocks):
+        for n in blocks:
+            vh[n] = matmul(nv[n].reshape(8 * TOK, 256), wc_blk[...]).astype(BF16).reshape(8, TOK, 1024)
+
+    values([place(d) for d in near])
+    wait_recv(nv.at[pl.ds(0, 5)], NORM_SIB)
+    values([place(d, 1) for d in near])
+
     wait_recv(lg_all, LOGITS)
     lg = lg_all[...].reshape(2, 8, TOK, 128)
     parts = swap_blocks([lg[:, s].reshape(2 * TOK, 128) for s in range(8)], TOK)
@@ -347,8 +366,14 @@
     prob = scaled / jnp.sum(scaled, axis=-1, keepdims=True)
     prob_scr[...] = prob
 
-    wait_recv(nv.at[other], NORM_SIB)
-    values((1 - core) * (N // 2))
+    away = (3, 4, 5)
+    wait_recv(nv.at[pl.ds(0, 3)], FAR)
+    for d in away:
+        block = nv.at[place(d)]
+        remote(block, block, FAR_SIB, S, sibling).start()
+    values([place(d) for d in away])
+    wait_recv(nv.at[pl.ds(0, 3)], FAR_SIB)
+    values([place(d, 1) for d in away])
 
     def head(ref, h):
         return [ref[:, g, :, h * 128 : (h + 1) * 128].reshape(256, 128) for g in range(8)]
@@ -367,9 +392,8 @@
         rsbuf[s] = parts[s // 2][start : start + TOK].astype(BF16)
     local(rsbuf.at[S], rsrx.at[S], GL_SUM)
 
-    @pl.loop(1, N)
-    def _(d):
-        s = (S + d) % N
+    for d in FAR_FIRST:
+        s = plane(d)
         remote(rsbuf.at[s], rsrx.at[S], GL_SUM, s, T).start()
 
     lines = po_all.at[y, top]
@@ -394,20 +418,19 @@
 
     wait_recv(rsrx, GL_SUM)
     gl_tile[...] = jnp.sum(rsrx[...].astype(F32), axis=0).astype(BF16)
-    place = gl_all.at[col, xpos]
+    target = gl_all.at[col, xpos]
     owner = row * NC + y
 
     @pl.when(y == col)
     def _():
-        local(gl_tile, place, GL)
+        local(gl_tile, target, GL)
 
     @pl.when(y != col)
     def _():
-        remote(gl_tile, place, GL, S, owner).start()
-
-    @pl.loop(1, N)
-    def _(d):
-        remote(gl_tile, place, GL, (S + d) % N, owner).start()
+        remote(gl_tile, target, GL, S, owner).start()
+
+    for d in FAR_FIRST:
+        remote(gl_tile, target, GL, plane(d), owner).start()
 
     wait_recv(po_all.at[pl.ds(0, 3), top], A2)
     wait_recv(po_all.at[pl.ds(0, 3), low], B2)
@@ -437,8 +460,10 @@
 
     wait_send(l_all.at[pl.ds(0, 15)], LEFT)
     wait_send(r_all.at[pl.ds(0, 8)], RIGHT_SIB)
-    wait_send(nv.at[pl.ds(0, 7)], NORM)
-    wait_send(nv.at[pl.ds(0, 8)], NORM_SIB)
+    wait_send(nv.at[pl.ds(0, 4)], NORM)
+    wait_send(nv.at[pl.ds(0, 5)], NORM_SIB)
+    wait_send(nv.at[pl.ds(0, 3)], FAR)
+    wait_send(nv.at[pl.ds(0, 3)], FAR_SIB)
     wait_send(lg_all.at[pl.ds(0, 15)], LOGITS)
     wait_send(po_all.at[0, pl.ds(0, 8), pl.ds(0, 48), :], A1)
     wait_send(po_all.at[0, pl.ds(0, 8), pl.ds(0, 48), :], B1)

time: 55.2 us -> 54.1 us (0.980)
  Pallas kernels: 54.1 us -> 53.1 us
    pallas_call x1, Pallas kernels: 49.2 us -> 48.2 us  [on_device(): pl.pallas_call(kernel, out_shape=[jax.ShapeDtypeStruct(grouped, BF16), ja...]
where the time goes in v4:
time: 54.1 us; the launch traced here: 53.7 us
  Pallas kernels  53.1 us (98%)
  between operations  0.64 us (1%)
    pallas_call x1, Pallas kernels, on_device(): pl.pallas_call(kernel, out_shape=[jax.ShapeDtypeStruct(grouped, BF16), ja...  48.2 us
    pallas_call x1, Pallas kernels, on_device(): pl.pallas_call(finish_kernel, grid=(NC,), out_shape=[jax.ShapeDtypeStruct...  4.87 us

profile of v4, /device:TPU:1, one launch (start us, length us, event | category | flops | bytes accessed | tf_op | source)
XLA Modules:
  0.0 53.7 jit_solution(16367770674664946816)
XLA Ops:
  0.6 48.2 %msa_block.1 = (bf16[8,4,16,64]{3,2,1,0:T(8,128)(2,1)}, bf16[4,16,64,128]{3,2,1,0:T(8,128)(2,1)}, bf16[4,4,16,128]{3,2,1,0:T(8,128)(2,1)}) custom-call(s32[256]{0:T(256)} %mask_s.1, bf16[8,4,16,64]{3,2,1,0:T(8,128)(2,1)} %bitcast.9, bf16[8,4,16,64]{3,2,1,0:T(8,128)(2,1)} %bitcast.10, bf16[32,64]{1,0:T(8,128)(2,1)} %bitcast.14, bf16[32,64]{1,0:T(8,128)(2,1)} %bitcast.15, ...), custom_call_target="tpu_custom_call" | custom-call | tf_op jit(solution)/shard_map/msa_block/pallas_call | solution.py:560
  48.9 4.9 %pair_gradient.1 = (bf16[8,4,16,64]{3,2,1,0:T(8,128)(2,1)}, bf16[64,64,128]{2,1,0:T(8,128)(2,1)}, bf16[64,64,128]{2,1,0:T(8,128)(2,1)}) custom-call(bf16[64,64,128]{2,1,0:T(8,128)(2,1)} %bitcast.8, bf16[4,4,16,128]{3,2,1,0:T(8,128)(2,1)} %get-tuple-element.10.gl_ref, f32[8,128]{1,0:T(8,128)} %bitcast.13, bf16[8,4,16,64]{3,2,1,0:T(8,128)(2,1)} %get-tuple-element.11.al_ref), custom_call_target="tpu_custom_call" | custom-call | tf_op jit(solution)/shard_map/pair_gradient/pallas_call | solution.py:589

commit v5 on v4

--- a/solution.py
+++ b/solution.py
@@ -74,7 +74,7 @@
     x_ref, adj_ref, w1_ref, w2_ref, wc_ref, ws_ref, wf_ref, score_ref, m_scr,
     xn_scr, lbuf, rbuf, l_all, r_all, nbuf, nv, vh, gbuf, gate_scr, wc_blk, wf_blk, m_hl,
     pin_tile, pin_scr, o_scr, p_scr, po_scr, po_tile, po_mid, po_all, lg_src, lg_all, prob_scr,
-    rsbuf, rsrx, gl_tile, gl_all,
+    al_scr, rsbuf, rsrx, gl_tile, gl_all,
     send_sem, recv_sem, local_sem,
 ):
     S = lax.axis_index("seq")
@@ -351,8 +351,12 @@
         remote(po_mid.at[low], own_b, B1, (S + NC * d) % N, T).start()
 
     def values(blocks):
-        for n in blocks:
-            vh[n] = matmul(nv[n].reshape(8 * TOK, 256), wc_blk[...]).astype(BF16).reshape(8, TOK, 1024)
+        for first in range(0, len(blocks), 2):
+            pair = blocks[first : first + 2]
+            rows = jnp.concatenate([nv[n].reshape(8 * TOK, 256) for n in pair], axis=0)
+            found = matmul(rows, wc_blk[...]).astype(BF16)
+            for k, n in enumerate(pair):
+                vh[n] = found[k * 128 : (k + 1) * 128].reshape(8, TOK, 1024)
 
     values([place(d) for d in near])
     wait_recv(nv.at[pl.ds(0, 5)], NORM_SIB)
@@ -414,7 +418,9 @@
     mixed = matmul_nt(jnp.concatenate(columns, axis=1), wf_blk[...])
     result = (by_group(x_ref[...].astype(F32)) + mixed).astype(BF16)
     for q in range(4):
-        out_al[:, q] = result[:, q * FEAT : (q + 1) * FEAT].reshape(8, TOK, FEAT)
+        al_scr[:, q] = result[:, q * FEAT : (q + 1) * FEAT].reshape(8, TOK, FEAT)
+    al_copy = pltpu.make_async_copy(al_scr, out_al, local_sem.at[10])
+    al_copy.start()
 
     wait_recv(rsrx, GL_SUM)
     gl_tile[...] = jnp.sum(rsrx[...].astype(F32), axis=0).astype(BF16)
@@ -437,7 +443,9 @@
     po_copy = pltpu.make_async_copy(po_all, out_pair, local_sem.at[9])
     po_copy.start()
     wait_recv(gl_all, GL)
-    out_gl[...] = gl_all[...]
+    gl_copy = pltpu.make_async_copy(gl_all, out_gl, local_sem.at[11])
+    gl_copy.start()
+    al_copy.wait()
     po_copy.wait()
 
     @pl.when(y == col)
@@ -470,31 +478,69 @@
     wait_send(po_all.at[pl.ds(0, 3), top], A2)
     wait_send(po_all.at[pl.ds(0, 3), low], B2)
     wait_send(rsrx.at[pl.ds(0, 15)], GL_SUM)
-
-
-def finish_kernel(po_ref, gl_ref, score_ref, al_ref, out_al, out_pair, out_grad, gl_scr, c_hl):
-    @pl.when(pl.program_id(0) == 0)
-    def _():
-        score = score_ref[...]
-        repeat = jnp.where(iota((HEADS, 128), 1) // TOK == iota((HEADS, 128), 0), 1.0, 0.0).astype(BF16)
-        high, low = split(score - jnp.mean(score, axis=1, keepdims=True))
-        c_hl[:128] = matmul_tn(high, repeat).astype(BF16)
-        c_hl[128:] = matmul_tn(low, repeat).astype(BF16)
-
-    out_al[...] = al_ref[...]
-    out_pair[...] = po_ref[...]
-    for s in range(NC):
-        gl_scr[:, s] = gl_ref[0, s].astype(F32).reshape(TOK, 1, 128)
+    gl_copy.wait()
+
+
+def finish_kernel(
+    po_hbm, gl_hbm, score_hbm, al_hbm, out_al, out_pair, out_grad,
+    po_ref, gl_ref, score_ref, al_ref, grad_ref, gl_scr, c_hl, sem,
+):
+    def chunk(ref, n):
+        return ref.at[pl.ds(n * TOK, TOK)]
+
+    def load(n):
+        return pltpu.make_async_copy(chunk(po_hbm, n), chunk(po_ref, n), sem.at[n])
+
+    def store(n):
+        return pltpu.make_async_copy(chunk(grad_ref, n), chunk(out_grad, n), sem.at[NC + n])
+
+    score_copy = pltpu.make_async_copy(score_hbm, score_ref, sem.at[2 * NC])
+    gl_copy = pltpu.make_async_copy(gl_hbm, gl_ref, sem.at[2 * NC + 1])
+    al_load = pltpu.make_async_copy(al_hbm, al_ref, sem.at[2 * NC + 2])
+    al_store = pltpu.make_async_copy(al_ref, out_al, sem.at[2 * NC + 3])
+
+    def keep(n):
+        return pltpu.make_async_copy(chunk(po_ref, n), chunk(out_pair, n), sem.at[2 * NC + 4 + n])
+
+    score_copy.start()
+    gl_copy.start()
+    for n in range(NC):
+        load(n).start()
+    al_load.start()
+
+    score_copy.wait()
+    score = score_ref[...]
+    repeat = jnp.where(iota((HEADS, 128), 1) // TOK == iota((HEADS, 128), 0), 1.0, 0.0).astype(BF16)
+    high, low = split(score - jnp.mean(score, axis=1, keepdims=True))
+    c_hl[:128] = matmul_tn(high, repeat).astype(BF16)
+    c_hl[128:] = matmul_tn(low, repeat).astype(BF16)
+    gl_copy.wait()
+    al_load.wait()
+    al_store.start()
+    for n in range(NC):
+        for s in range(NC):
+            gl_scr[n * TOK : (n + 1) * TOK, s] = gl_ref[n, s].astype(F32).reshape(TOK, 1, 128)
     own = (iota((1, 1, TOK, 128), 3) % TOK) == iota((1, 1, TOK, 128), 2)
     part = TOK // 2
-    for b in range(2):
-        rows = pl.ds(b * part, part)
-        normal, inverse = normalize(po_ref[rows].reshape(part * 64, 128).astype(F32))
-        lhs = jnp.where(own, gl_scr[rows], 0.0).astype(BF16).reshape(part * 64, 128)
-        grad = matmul_nt(lhs, c_hl[...])
-        grad = grad[:, :128] + grad[:, 128:]
-        along = jnp.mean(grad * normal, axis=-1, keepdims=True)
-        out_grad[rows] = (inverse * (grad - normal * along)).astype(BF16).reshape(part, 64, 128)
+
+    @pl.loop(0, NC)
+    def _(n):
+        load(n).wait()
+        keep(n).start()
+        for b in range(2):
+            rows = pl.ds(n * TOK + b * part, part)
+            normal, inverse = normalize(po_ref[rows].reshape(part * 64, 128).astype(F32))
+            lhs = jnp.where(own, gl_scr[rows], 0.0).astype(BF16).reshape(part * 64, 128)
+            grad = matmul_nt(lhs, c_hl[...])
+            grad = grad[:, :128] + grad[:, 128:]
+            along = jnp.mean(grad * normal, axis=-1, keepdims=True)
+            grad_ref[rows] = (inverse * (grad - normal * along)).astype(BF16).reshape(part, 64, 128)
+        store(n).start()
+
+    for n in range(NC):
+        store(n).wait()
+        keep(n).wait()
+    al_store.wait()
 
 
 def on_device(
@@ -510,7 +556,6 @@
     final_mixing_weights,
     adjoint_of_rowset,
 ):
-    vmem = pl.BlockSpec(memory_space=pltpu.VMEM)
     smem = pl.BlockSpec(memory_space=pltpu.SMEM)
     hbm = pl.BlockSpec(memory_space=pltpu.HBM)
     V = pltpu.VMEM
@@ -548,13 +593,14 @@
         V((TOK, 128), F32),
         V((N, TOK, 128), F32),
         V((HEADS, TOK, 256), F32),
+        V((8, 4, TOK, FEAT), BF16),
         V((N, TOK, 128), BF16),
         V((N, TOK, 128), BF16),
         V((TOK, 128), BF16),
         V((NC, NC, TOK, 128), BF16),
         pltpu.SemaphoreType.DMA((PHASES,)),
         pltpu.SemaphoreType.DMA((PHASES,)),
-        pltpu.SemaphoreType.DMA((10,)),
+        pltpu.SemaphoreType.DMA((12,)),
     ]
     grouped = (8, 4, TOK, FEAT)
     aligned, pair_block, grad_logits = pl.pallas_call(
@@ -565,7 +611,7 @@
             jax.ShapeDtypeStruct((NC, NC, TOK, 128), BF16),
         ],
         in_specs=[smem] + [hbm] * 10,
-        out_specs=[vmem, hbm, vmem],
+        out_specs=[hbm, hbm, hbm],
         scratch_shapes=scratch,
         compiler_params=pltpu.CompilerParams(
             collective_id=0, has_side_effects=True, vmem_limit_bytes=60 * 1024 * 1024
@@ -584,24 +630,25 @@
         outer_matrix,
         pair_input,
     )
-    rows = pl.BlockSpec((TOK, 64, 128), lambda n: (n, 0, 0))
-    groups = pl.BlockSpec((2, 4, TOK, FEAT), lambda n: (n, 0, 0, 0))
     aligned, pair_output, pair_gradient = pl.pallas_call(
         finish_kernel,
-        grid=(NC,),
         out_shape=[
             jax.ShapeDtypeStruct(grouped, BF16),
             jax.ShapeDtypeStruct((64, 64, 128), BF16),
             jax.ShapeDtypeStruct((64, 64, 128), BF16),
         ],
-        in_specs=[
-            rows,
-            pl.BlockSpec((1, NC, TOK, 128), lambda n: (n, 0, 0, 0)),
-            pl.BlockSpec((HEADS, 128), lambda n: (0, 0)),
-            groups,
+        in_specs=[hbm] * 4,
+        out_specs=[hbm] * 3,
+        scratch_shapes=[
+            V((64, 64, 128), BF16),
+            V((NC, NC, TOK, 128), BF16),
+            V((HEADS, 128), F32),
+            V(grouped, BF16),
+            V((64, 64, 128), BF16),
+            V((64, NC, 1, 128), F32),
+            V((256, 128), BF16),
+            pltpu.SemaphoreType.DMA((3 * NC + 4,)),
         ],
-        out_specs=[groups, rows, rows],
-        scratch_shapes=[V((TOK, NC, 1, 128), F32), V((256, 128), BF16)],
         compiler_params=pltpu.CompilerParams(vmem_limit_bytes=60 * 1024 * 1024),
         name="pair_gradient",
     )(pair_block.reshape(64, 64, 128), grad_logits, score_matrix.T, aligned)

time: 54.1 us -> 53.4 us (0.987)
  Pallas kernels: 53.1 us -> 52.2 us
    pallas_call x1, Pallas kernels: 4.87 us -> 4.3 us  [on_device(): pl.pallas_call(finish_kernel, out_shape=[jax.ShapeDtypeStruct(grouped, BF...]
where the time goes in v5:
time: 53.4 us; the launch traced here: 52.8 us
  Pallas kernels  52.2 us (98%)
  between operations  0.64 us (1%)
    pallas_call x1, Pallas kernels, on_device(): pl.pallas_call(kernel, out_shape=[jax.ShapeDtypeStruct(grouped, BF16), ja...  47.9 us
    pallas_call x1, Pallas kernels, on_device(): pl.pallas_call(finish_kernel, out_shape=[jax.ShapeDtypeStruct(grouped, BF...  4.3 us

profile of v5, /device:TPU:1, one launch (start us, length us, event | category | flops | bytes accessed | tf_op | source)
XLA Modules:
  0.0 52.8 jit_solution(11766838467067946229)
XLA Ops:
  0.6 47.9 %msa_block.1 = (bf16[8,4,16,64]{3,2,1,0:T(8,128)(2,1)}, bf16[4,16,64,128]{3,2,1,0:T(8,128)(2,1)}, bf16[4,4,16,128]{3,2,1,0:T(8,128)(2,1)}) custom-call(s32[256]{0:T(256)} %mask_s.1, bf16[8,4,16,64]{3,2,1,0:T(8,128)(2,1)} %bitcast.9, bf16[8,4,16,64]{3,2,1,0:T(8,128)(2,1)} %bitcast.10, bf16[32,64]{1,0:T(8,128)(2,1)} %bitcast.14, bf16[32,64]{1,0:T(8,128)(2,1)} %bitcast.15, ...), custom_call_target="tpu_custom_call" | custom-call | tf_op jit(solution)/shard_map/msa_block/pallas_call | solution.py:606
  48.5 4.3 %pair_gradient.1 = (bf16[8,4,16,64]{3,2,1,0:T(8,128)(2,1)}, bf16[64,64,128]{2,1,0:T(8,128)(2,1)}, bf16[64,64,128]{2,1,0:T(8,128)(2,1)}) custom-call(bf16[64,64,128]{2,1,0:T(8,128)(2,1)} %bitcast.8, bf16[4,4,16,128]{3,2,1,0:T(8,128)(2,1)} %get-tuple-element.10.gl_hbm, f32[8,128]{1,0:T(8,128)} %bitcast.13, bf16[8,4,16,64]{3,2,1,0:T(8,128)(2,1)} %get-tuple-element.11.al_hbm), custom_call_target="tpu_custom_call" | custom-call | tf_op jit(solution)/shard_map/pair_gradient/pallas_call | solution.py:633
